TPU v7x, 128 devices: a whole 4x4x4 slice. The times are simulated.
128 devices in a mesh: dp: 16 (over y, x), row: 2 (over core), col: 4 (over z).
Axes of the slice: x: 4, y: 4, z: 4, core: 2. Of those that a mesh axis runs over, the one named last changes fastest.
Arguments:
- tokens_in: bfloat16 [2048, 6144], P('dp', 'row'), may hold values from -6 to 6
- out_grad: bfloat16 [2048, 6144], P('dp', 'row'), may hold values from -6 to 6
- up_weight: bfloat16 [2, 4, 288, 128, 128], P('row', 'col'), may hold values from -0.15625 to 0.15625
- down_weight: bfloat16 [2, 4, 288, 128, 128], P('row', 'col'), may hold values from -0.15625 to 0.15625
- up_blocks: int32 [2, 4, 288], P('row', 'col'), may hold values from 0 to 1151, as said below
- down_blocks: int32 [2, 4, 288], P('row', 'col'), may hold values from 0 to 1151, as said below
- owners: int32 [2, 4, 288], P('row', 'col'), may hold values from 0 to 287, as said below
Outputs:
- input_grad: bfloat16 [2048, 6144], P(('dp', 'col'), 'row')
- up_grad: bfloat16 [2, 4, 288, 128, 128], P('row', 'col', 'dp')
- down_grad: bfloat16 [2, 4, 288, 128, 128], P('row', 'col', 'dp')
Inputs may be any that keep to these rules, and one draw needn't show every extreme that they name: `up_blocks`: within each cell the entries are distinct; their number is 288. `down_blocks`: within each cell the entries are distinct; their number is 288. `owners`: within each cell the entries are a permutation of the slots.
All inputs are finite; a program needn't handle non-finite values.
Results may differ from a plain program's by a relative error of at most 0.024.
Values may be sent and summed in bfloat16 or wider, within the bound.
A program may use at most 192 MiB of HBM per device.

v0:
```python
import jax
import jax.numpy as jnp
from jax import lax
from jax.sharding import PartitionSpec as P

H = 24576


root_two_pi = 0.7978845608028654
cubic_coef = 0.044715


def activate(pre_sum, back_sum):
    inner_arg = root_two_pi * (pre_sum + cubic_coef * pre_sum * pre_sum * pre_sum)
    tanh_inner = jnp.tanh(inner_arg)
    gelu_value = 0.5 * pre_sum * (1.0 + tanh_inner)
    gelu_slope = 0.5 * (1.0 + tanh_inner) + 0.5 * pre_sum * (
        1.0 - tanh_inner * tanh_inner
    ) * root_two_pi * (1.0 + 3.0 * cubic_coef * pre_sum * pre_sum)
    return (gelu_value.astype(jnp.bfloat16), (back_sum * gelu_slope).astype(jnp.bfloat16))


def one_hot_table(picks, width):
    return (picks[:, None] == jnp.arange(width, dtype=jnp.int32)[None, :]).astype(jnp.bfloat16)


def select_blocks(left3, table):
    return jnp.einsum("tjb,kj->tkb", left3, table, preferred_element_type=jnp.float32).astype(
        jnp.bfloat16
    )


def place_blocks(left3, weights, table_in, table_out, transposed):
    picked = select_blocks(left3, table_in)
    if transposed:
        product = jnp.einsum("tkb,kcb->tkc", picked, weights, preferred_element_type=jnp.float32)
    else:
        product = jnp.einsum("tkb,kbc->tkc", picked, weights, preferred_element_type=jnp.float32)
    return jnp.einsum(
        "tkc,kw->twc",
        product,
        table_out.astype(jnp.float32),
        precision=lax.Precision.HIGHEST,
        preferred_element_type=jnp.float32,
    )


def block_grads(left3, right3, table_left, table_right):
    left_blocks = select_blocks(left3, table_left)
    right_blocks = select_blocks(right3, table_right)
    return jnp.einsum("tkb,tkc->kbc", left_blocks, right_blocks, preferred_element_type=jnp.float32)


def shards(tokens_in, out_grad, up_weight, down_weight, up_blocks, down_blocks, owners):
    block_size = up_weight.shape[-1]
    row_count = tokens_in.shape[0]
    cell_rows = tokens_in.shape[1] // block_size
    cell_cols = H // (block_size * lax.axis_size("col"))
    up_local = up_weight[0, 0]
    down_local = down_weight[0, 0]
    up_index = up_blocks[0, 0]
    down_index = down_blocks[0, 0]
    up_feat = up_index // cell_cols
    up_hid = up_index % cell_cols
    down_hid = down_index // cell_rows
    down_feat = down_index % cell_rows
    up_feat_table = one_hot_table(up_feat, cell_rows)
    up_hid_table = one_hot_table(up_hid, cell_cols)
    down_feat_table = one_hot_table(down_feat, cell_rows)
    down_hid_table = one_hot_table(down_hid, cell_cols)
    inputs3 = tokens_in.reshape(row_count, cell_rows, block_size)
    grads3 = out_grad.reshape(row_count, cell_rows, block_size)
    pre_part = place_blocks(inputs3, up_local, up_feat_table, up_hid_table, False).reshape(
        row_count, -1
    )
    back_part = place_blocks(grads3, down_local, down_feat_table, down_hid_table, True).reshape(
        row_count, -1
    )
    pre_sum, back_sum = (
        lax.psum(pre_part.astype(jnp.bfloat16), "row").astype(jnp.float32),
        lax.psum(back_part.astype(jnp.bfloat16), "row").astype(jnp.float32),
    )
    hidden, pre_grad = activate(pre_sum, back_sum)
    hidden3 = hidden.reshape(row_count, cell_cols, block_size)
    pre_grad3 = pre_grad.reshape(row_count, cell_cols, block_size)
    input_grad = lax.psum_scatter(
        place_blocks(pre_grad3, up_local, up_hid_table, up_feat_table, True)
        .reshape(lax.axis_size("col") * (row_count // lax.axis_size("col")), -1)
        .astype(jnp.bfloat16),
        "col",
        scatter_dimension=0,
        tiled=True,
    )
    owner_order = jnp.argsort(owners[0, 0])
    up_term = block_grads(inputs3, pre_grad3, up_feat_table[owner_order], up_hid_table[owner_order])
    down_term = block_grads(
        hidden3, grads3, down_hid_table[owner_order], down_feat_table[owner_order]
    )
    up_grad, down_grad = (
        lax.psum_scatter(
            up_term.astype(jnp.bfloat16), "dp", scatter_dimension=0, tiled=True
        ).astype(jnp.float32),
        lax.psum_scatter(
            down_term.astype(jnp.bfloat16), "dp", scatter_dimension=0, tiled=True
        ).astype(jnp.float32),
    )
    return (
        input_grad,
        up_grad.astype(jnp.bfloat16)[None, None],
        down_grad.astype(jnp.bfloat16)[None, None],
    )


def solution(mesh):
    placed = (
        P("dp", "row"),
        P("dp", "row"),
        P("row", "col", None, None, None),
        P("row", "col", None, None, None),
        P("row", "col", None),
        P("row", "col", None),
        P("row", "col", None),
    )
    return jax.shard_map(
        shards,
        mesh=mesh,
        in_specs=placed,
        out_specs=(
            P(("dp", "col"), "row"),
            P("row", "col", "dp", None, None),
            P("row", "col", "dp", None, None),
        ),
        check_vma=False,
    )
```

profile of v0, /device:TPU:1, one launch (start us, length us, event | category | flops | bytes accessed | tf_op | source)
XLA Modules:
  0.0 405.7 jit_solution(2475628452141702724)
XLA Ops:
  12.6 5.2 %fusion.78 = bf16[288,128,128]{2,0,1:T(8,128)(2,1)} fusion(bf16[128,24,128]{2,1,0:T(8,128)(2,1)S(1)} %bitcast.116, s32[288]{0:T(512)S(1)} %get-tuple-element.16), kind=kOutput, calls=%fused_computation.82 | convolution fusion | flops 226499328 | bytes 10224768 | tf_op jit(solution)/shard_map/tjb,kj->tkb/dot_general | solution.py:28
  17.8 18.4 %fusion.13 = f32[288,128,128]{2,1,0:T(8,128)} fusion(bf16[288,128,128]{2,0,1:T(8,128)(2,1)} %fusion.78, bf16[1,1,288,128,128]{4,3,2,1,0:T(8,128)(2,1)} %param.9), kind=kOutput, calls=%fused_computation.21 | convolution fusion | flops 1207959552 | bytes 37748736 | tf_op jit(solution)/shard_map/tkb,kbc->tkc/dot_general | solution.py:38
  36.2 23.9 %fusion.55 = bf16[48,128,128]{2,0,1:T(8,128)(2,1)S(1)} fusion(f32[288,128,128]{2,1,0:T(8,128)} %fusion.13, s32[288]{0:T(512)S(1)} %get-tuple-element.15), kind=kOutput, calls=%fused_computation.56 | convolution fusion | flops 2718709248 | bytes 20448384 | tf_op jit(solution)/shard_map/tkc,kw->twc/dot_general | solution.py:39
  60.1 5.2 %fusion.71 = bf16[288,128,128]{2,0,1:T(8,128)(2,1)} fusion(bf16[128,24,128]{2,1,0:T(8,128)(2,1)S(1)} %bitcast.114, s32[288]{0:T(512)S(1)} %get-tuple-element.14), kind=kOutput, calls=%fused_computation.75 | convolution fusion | flops 226499328 | bytes 10224768 | tf_op jit(solution)/shard_map/tjb,kj->tkb/dot_general | solution.py:28
  65.2 16.2 %fusion.10 = f32[288,128,128]{2,1,0:T(8,128)} fusion(bf16[288,128,128]{2,0,1:T(8,128)(2,1)} %fusion.71, bf16[1,1,288,128,128]{4,3,2,1,0:T(8,128)(2,1)} %param.10), kind=kOutput, calls=%fused_computation.19 | convolution fusion | flops 1207959552 | bytes 37748736 | tf_op jit(solution)/shard_map/tkb,kcb->tkc/dot_general | solution.py:36
  81.4 23.7 %fusion.52 = bf16[48,128,128]{2,0,1:T(8,128)(2,1)S(1)} fusion(f32[288,128,128]{2,1,0:T(8,128)} %fusion.10, s32[288]{0:T(512)S(1)} %get-tuple-element.13), kind=kOutput, calls=%fused_computation.55 | convolution fusion | flops 2718709248 | bytes 20448384 | tf_op jit(solution)/shard_map/tkc,kw->twc/dot_general | solution.py:39
  105.1 2.4 copy_bitcast_fusion
  107.6 3.8 sort.17
  111.5 1.4 gather_fusion.1
  114.3 5.0 %fusion.69 = bf16[288,128,128]{2,0,1:T(8,128)(2,1)} fusion(bf16[128,24,128]{2,1,0:T(8,128)(2,1)S(1)} %bitcast.117, pred[288,24]{1,0:T(32,128)(4,1)S(1)} %gather_fusion), kind=kOutput, calls=%fused_computation.73 | convolution fusion | flops 226492416 | bytes 10230528 | tf_op jit(solution)/shard_map/tjb,kj->tkb/dot_general | solution.py:28
  119.3 12.9 %copy.16 = bf16[288,128,128]{1,2,0:T(8,128)(2,1)} copy(bf16[288,128,128]{2,0,1:T(8,128)(2,1)} %fusion.69) | data formatting | bytes 18874368 | tf_op jit(solution)/shard_map/tjb,kj->tkb/dot_general | solution.py:28
  132.1 8.0 %all-reduce.3.cloned.1.call-done = (bf16[128,6144]{1,0:T(8,128)(2,1)}, bf16[128,6144]{1,0:T(8,128)(2,1)}) async-done(((bf16[128,6144]{1,0:T(8,128)(2,1)}, bf16[128,6144]{1,0:T(8,128)(2,1)}), (bf16[128,6144]{1,0:T(8,128)(2,1)}, bf16[128,6144]{1,0:T(8,128)(2,1)})) %all-reduce.3.cloned.1.call-update) | async-done | bytes 3145744 | tf_op jit(solution)/shard_map/psum | solution.py:80
  140.2 3.8 fusion.58
  144.4 5.1 %fusion.74 = bf16[288,128,128]{2,0,1:T(8,128)(2,1)} fusion(bf16[128,48,128]{2,1,0:T(8,128)(2,1)S(1)} %bitcast.112, s32[288]{0:T(512)S(1)} %get-tuple-element.15), kind=kOutput, calls=%fused_computation.78 | convolution fusion | flops 452998656 | bytes 11011200 | tf_op jit(solution)/shard_map/tjb,kj->tkb/dot_general | solution.py:28
  149.5 5.0 %fusion.67 = bf16[288,128,128]{2,0,1:T(8,128)(2,1)} fusion(bf16[128,48,128]{2,1,0:T(8,128)(2,1)S(1)} %bitcast.113, pred[288,48]{1,0:T(32,128)(4,1)S(1)} %gather_fusion.1), kind=kOutput, calls=%fused_computation.71 | convolution fusion | flops 452984832 | bytes 11023872 | tf_op jit(solution)/shard_map/tjb,kj->tkb/dot_general | solution.py:28
  154.5 15.7 %fusion.16 = f32[288,128,128]{2,1,0:T(8,128)} fusion(bf16[288,128,128]{2,0,1:T(8,128)(2,1)} %fusion.74, bf16[1,1,288,128,128]{4,3,2,1,0:T(8,128)(2,1)} %param.9), kind=kOutput, calls=%fused_computation.23 | convolution fusion | flops 1207959552 | bytes 37748736 | tf_op jit(solution)/shard_map/tkb,kcb->tkc/dot_general | solution.py:36
  170.2 22.7 %fusion.60 = bf16[24,128,128]{2,0,1:T(8,128)(2,1)S(1)} fusion(f32[288,128,128]{2,1,0:T(8,128)} %fusion.16, s32[288]{0:T(512)S(1)} %get-tuple-element.16), kind=kOutput, calls=%fused_computation.61 | convolution fusion | flops 1359354624 | bytes 19661952 | tf_op jit(solution)/shard_map/tkc,kw->twc/dot_general | solution.py:39
  194.1 16.1 %fusion.36 = bf16[288,128,128]{2,1,0:T(8,128)(2,1)} fusion(bf16[288,128,128]{2,0,1:T(8,128)(2,1)} %fusion.67, bf16[288,128,128]{1,2,0:T(8,128)(2,1)} %copy.16), kind=kOutput, calls=%fused_computation.43 | convolution fusion | flops 1212678144 | bytes 28311552 | tf_op jit(solution)/shard_map/tkb,tkc->kbc/dot_general | solution.py:51
  213.0 5.1 %fusion.63 = bf16[288,128,128]{2,0,1:T(8,128)(2,1)} fusion(bf16[128,24,128]{2,1,0:T(8,128)(2,1)S(1)} %bitcast.115, pred[288,24]{1,0:T(32,128)(4,1)S(1)} %gather_fusion.3), kind=kOutput, calls=%fused_computation.67 | convolution fusion | flops 226492416 | bytes 10230528 | tf_op jit(solution)/shard_map/tjb,kj->tkb/dot_general | solution.py:28
  218.4 5.1 %fusion.65 = bf16[288,128,128]{2,0,1:T(8,128)(2,1)} fusion(bf16[128,48,128]{2,1,0:T(8,128)(2,1)S(1)} %bitcast.118, pred[288,48]{1,0:T(32,128)(4,1)S(1)} %gather_fusion.2), kind=kOutput, calls=%fused_computation.69 | convolution fusion | flops 452984832 | bytes 11023872 | tf_op jit(solution)/shard_map/tjb,kj->tkb/dot_general | solution.py:28
  223.5 13.5 %copy.18 = bf16[288,128,128]{1,2,0:T(8,128)(2,1)} copy(bf16[288,128,128]{2,0,1:T(8,128)(2,1)} %fusion.65) | data formatting | bytes 18874368 | tf_op jit(solution)/shard_map/tjb,kj->tkb/dot_general | solution.py:28
  237.0 16.1 %fusion.31 = bf16[288,128,128]{2,1,0:T(8,128)(2,1)} fusion(bf16[288,128,128]{2,0,1:T(8,128)(2,1)} %fusion.63, bf16[288,128,128]{1,2,0:T(8,128)(2,1)} %copy.18), kind=kOutput, calls=%fused_computation.42 | convolution fusion | flops 1212678144 | bytes 28311552 | tf_op jit(solution)/shard_map/tkb,tkc->kbc/dot_general | solution.py:51
  253.1 55.1 %reduce-scatter.6.cloned.1.call-done = bf16[18,128,128]{2,1,0:T(8,128)(2,1)} async-done(((bf16[288,128,128]{2,1,0:T(8,128)(2,1)}), bf16[18,128,128]{2,1,0:T(8,128)(2,1)}) %reduce-scatter.6.cloned.1.call-update) | async-done | bytes 589840 | tf_op jit(solution)/shard_map/reduce_scatter | solution.py:100
  308.2 90.6 %reduce-scatter.8.cloned.1.call-done = bf16[18,128,128]{2,1,0:T(8,128)(2,1)} async-done(((bf16[288,128,128]{2,1,0:T(8,128)(2,1)}), bf16[18,128,128]{2,1,0:T(8,128)(2,1)}) %reduce-scatter.8.cloned.1.call-update) | async-done | bytes 589840 | tf_op jit(solution)/shard_map/reduce_scatter | solution.py:103
  (33 shorter events, 11.6 us)
Async XLA Ops:
  7.2 133.0 %all-reduce.3.cloned.1.call-start = ((), (), s32[]{:S(2)}) async-start(), calls=%async_computation.6 | async-start | bytes 6291456 | tf_op jit(solution)/shard_map/psum | solution.py:80
  105.1 2.5 copy-start
  107.5 145.6 %reduce-scatter.4.cloned.1.call-start = ((), (), s32[]{:S(2)}) async-start(), calls=%async_computation.3 | async-start | bytes 983040 | tf_op jit(solution)/shard_map/reduce_scatter | solution.py:86
  194.0 114.2 %reduce-scatter.6.cloned.1.call-start = ((), (), s32[]{:S(2)}) async-start(), calls=%async_computation.4 | async-start | bytes 10027008 | tf_op jit(solution)/shard_map/reduce_scatter | solution.py:100
  210.2 188.5 %reduce-scatter.8.cloned.1.call-start = ((), (), s32[]{:S(2)}) async-start(), calls=%async_computation.5 | async-start | bytes 10027008 | tf_op jit(solution)/shard_map/reduce_scatter | solution.py:103
Sparse Core Ops, SparseCore 0:
  107.6 32.4 all-reduce.2
  194.1 22.4 reduce-scatter.3
  221.2 86.9 reduce-scatter.5
  312.1 86.6 reduce-scatter.7
where the time goes:
time: 412 us; the launch traced here: 406 us
  matrix products  188 us (46%)
  waiting for transfers between devices  154 us (37%)
  local copies, waits for them, and re-layouts  38.1 us (9%)
  between operations  14.4 us (3%)
  other arithmetic  10.9 us (3%)
    reduce_scatter x1, waiting for transfers between devices, shards(): lax.psum_scatter(down_term.astype(jnp.bfloat16), 'dp', scatter_dimension=...  90.6 us
    dot_general x3, matrix products, place_blocks(): jnp.einsum('tkc,kw->twc', product, table_out.astype(jnp.float32), precisi...  70.3 us
    reduce_scatter x1, waiting for transfers between devices, shards(): lax.psum_scatter(up_term.astype(jnp.bfloat16), 'dp', scatter_dimension=0,...  55.1 us
    dot_general x7, matrix products, select_blocks(): jnp.einsum('tjb,kj->tkb', left3, table, preferred_element_type=jnp.float32)  35.6 us
    dot_general x2, matrix products, block_grads(): jnp.einsum('tkb,tkc->kbc', left_blocks, right_blocks, preferred_element_t...  32.2 us
    dot_general x2, matrix products, place_blocks(): jnp.einsum('tkb,kcb->tkc', picked, weights, preferred_element_type=jnp.fl...  31.9 us
    dot_general x2, local copies, waits for them, and re-layouts, select_blocks(): jnp.einsum('tjb,kj->tkb', left3, table, preferred_element_type=jnp.float32)  26.3 us
    dot_general x1, matrix products, place_blocks(): jnp.einsum('tkb,kbc->tkc', picked, weights, preferred_element_type=jnp.fl...  18.4 us
  transfers between devices with their start and end apart: 4, of which 3 were waited for; matrix products, arithmetic and copies ran while one was open for 21% of the time, Pallas kernels for 0%

commit v1 on v0

v1 whole, which is shorter than its diff:
```python
import functools

import jax
import jax.numpy as jnp
from jax import lax
from jax.experimental import pallas as pl
from jax.experimental.pallas import tpu as pltpu
from jax.sharding import PartitionSpec as P

BF = jnp.bfloat16
F32 = jnp.float32
B = 128
ROWS = 24
COLS = 48
NBLK = 288
SIDE = 4
SHARE = 18
CH = 12
NN = (((1,), (0,)), ((), ()))
NT = (((1,), (1,)), ((), ()))
MESH = pl.DeviceIdType.MESH

root_two_pi = 0.7978845608028654
cubic_coef = 0.044715


def activate(pre_sum, back_sum):
    square = pre_sum * pre_sum
    inner_arg = root_two_pi * (pre_sum + cubic_coef * square * pre_sum)
    tanh_inner = jnp.tanh(inner_arg)
    half = 0.5 * (1.0 + tanh_inner)
    slope = half + 0.5 * pre_sum * (1.0 - tanh_inner * tanh_inner) * root_two_pi * (
        1.0 + 3.0 * cubic_coef * square
    )
    return pre_sum * half, back_sum * slope


def dot(left, right, dims):
    return lax.dot_general(left, right, dims, preferred_element_type=F32)


def lanes(index):
    return pl.ds(pl.multiple_of(index * B, B), B)


def forward_kernel(
    steps, unroll, uf, uh, df, dh, x_ref, g_ref, wu_ref, wd_ref, pre_ref, back_ref, xt_ref, gb_ref, pacc, bacc
):
    step = pl.program_id(0)
    chunk = wu_ref.shape[0]

    @pl.when(step == 0)
    def _():
        pacc[...] = jnp.zeros_like(pacc)
        bacc[...] = jnp.zeros_like(bacc)
        for f in range(ROWS):
            xt_ref[f] = x_ref[:, f * B : (f + 1) * B].T
            gb_ref[f] = g_ref[:, f * B : (f + 1) * B]

    def group(i, carry):
        ups, downs = [], []
        for j in range(unroll):
            k = step * chunk + i * unroll + j
            ups.append((uh[k], dot(x_ref[:, lanes(uf[k])], wu_ref[i * unroll + j], NN)))
            downs.append((dh[k], dot(g_ref[:, lanes(df[k])], wd_ref[i * unroll + j], NT)))
        for j in range(unroll):
            pacc[ups[j][0]] += ups[j][1]
            bacc[downs[j][0]] += downs[j][1]
        return carry

    lax.fori_loop(0, chunk // unroll, group, 0)

    @pl.when(step == steps - 1)
    def _():
        pre_ref[...] = pacc[...].astype(BF)
        back_ref[...] = bacc[...].astype(BF)


def forward(uf, uh, df, dh, x, g, wu, wd, steps=12, unroll=12):
    chunk = NBLK // steps

    def whole(shape):
        return pl.BlockSpec(shape, lambda s, *_: (0,) * len(shape))

    weights = pl.BlockSpec((chunk, B, B), lambda s, *_: (s, 0, 0))
    return pl.pallas_call(
        functools.partial(forward_kernel, steps, unroll),
        grid_spec=pltpu.PrefetchScalarGridSpec(
            num_scalar_prefetch=4,
            grid=(steps,),
            in_specs=[whole((B, ROWS * B)), whole((B, ROWS * B)), weights, weights],
            out_specs=[whole((COLS, B, B)), whole((COLS, B, B)), whole((ROWS, B, B)), whole((ROWS, B, B))],
            scratch_shapes=[pltpu.VMEM((COLS, B, B), F32), pltpu.VMEM((COLS, B, B), F32)],
        ),
        out_shape=[
            jax.ShapeDtypeStruct((COLS, B, B), BF),
            jax.ShapeDtypeStruct((COLS, B, B), BF),
            jax.ShapeDtypeStruct((ROWS, B, B), BF),
            jax.ShapeDtypeStruct((ROWS, B, B), BF),
        ],
        compiler_params=pltpu.CompilerParams(vmem_limit_bytes=48 * 2**20),
        name="forward",
    )(uf, uh, df, dh, x, g, wu, wd)


def back_kernel(*refs):
    (gu_f, gu_h, gd_f, gd_h, sx_h, sx_k, keep, last, some) = refs[:9]
    pre_ref, back_ref, xt_own, og_own, wu_hbm = refs[9:14]
    dx_out, up_out, dn_out = refs[14:17]
    (
        pre_in, back_in, pg_own, ht_own,
        xt_l, xt_r, xt_o, og_l, og_r, og_o,
        pg_l, pg_r, pg_o, ht_l, ht_r, ht_o,
        wu, runs, dxp, zin,
        uf_s, ur_s, ul_s, ua_t, ub_t, ul_v, ur_v, u_acc,
        df_s, dr_s, dl_s, da_t, db_t, dl_v, dr_v, d_acc,
        ex_s, ex_r, ag_s, ag_r, pa_s, pa_r, rs_s, rs_r, z_s, z_r, w_s,
    ) = refs[17:]
    dp, row, col = lax.axis_index("dp"), lax.axis_index("row"), lax.axis_index("col")
    y, x = dp // SIDE, dp % SIDE
    other = (dp, 1 - row, col)
    x_right = (y * SIDE + (x + 1) % SIDE, row, col)
    x_left = (y * SIDE + (x + 3) % SIDE, row, col)
    y_right = (((y + 1) % SIDE) * SIDE + x, row, col)
    y_left = (((y + 3) % SIDE) * SIDE + x, row, col)
    z_peers = [(dp, row, (col + d) % SIDE) for d in range(1, SIDE)]

    barrier = pltpu.get_barrier_semaphore()
    peers = [other, x_right, x_left, y_right, y_left] + z_peers
    for peer in peers:
        pl.semaphore_signal(barrier, inc=1, device_id=peer, device_id_type=MESH)
    pl.semaphore_wait(barrier, len(peers))

    started = []

    def send(src, dst, send_sem, recv_sem, peer):
        copy = pltpu.make_async_remote_copy(
            src_ref=src, dst_ref=dst, send_sem=send_sem, recv_sem=recv_sem, device_id=peer, device_id_type=MESH
        )
        copy.start()
        started.append(copy)

    def arrived(dst, send_sem, recv_sem, peer):
        pltpu.make_async_remote_copy(
            src_ref=dst, dst_ref=dst, send_sem=send_sem, recv_sem=recv_sem, device_id=peer, device_id_type=MESH
        ).wait_recv()

    for c in range(2):
        theirs = pl.ds((1 - row) * ROWS + c * CH, CH)
        here = pl.ds(c * CH, CH)
        send(pre_ref.at[theirs], pre_in.at[here], ex_s.at[c], ex_r.at[c], other)
        send(back_ref.at[theirs], back_in.at[here], ex_s.at[2 + c], ex_r.at[2 + c], other)

    weights = pltpu.make_async_copy(wu_hbm, wu, w_s)
    weights.start()

    kinds = {
        "xt": (0, xt_own, xt_l, xt_r, xt_o, x_right, x_left, 0),
        "og": (1, og_own, og_l, og_r, og_o, y_right, y_left, 0),
        "pg": (2, pg_own, pg_l, pg_r, pg_o, x_right, x_left, row * ROWS),
        "ht": (3, ht_own, ht_l, ht_r, ht_o, y_right, y_left, row * ROWS),
    }

    def part(base, c):
        return pl.ds(base + c * CH, CH)

    def ring_out(kind, c, way):
        n, own, left, right, _, to_right, to_left, base = kinds[kind]
        at = part(base, c)
        if way == "r":
            send(own.at[at], left.at[at], ag_s.at[n, c], ag_r.at[n, c], to_right)
        else:
            send(own.at[at], right.at[at], ag_s.at[n, 2 + c], ag_r.at[n, 2 + c], to_left)

    def ring_wait(kind, slot):
        n, _, left, right, far, to_right, to_left, base = kinds[kind]
        dst = (left, left, right, right, far, far)[slot].at[part(base, slot % 2)]
        arrived(dst, ag_s.at[n, slot], ag_r.at[n, slot], to_right)

    def ring_forward(kind, way):
        n, _, left, right, far, to_right, to_left, base = kinds[kind]
        if way == "r":
            at = part(base, 0)
            send(left.at[at], far.at[at], ag_s.at[n, 4], ag_r.at[n, 4], to_right)
        else:
            at = part(base, 1)
            send(right.at[at], far.at[at], ag_s.at[n, 5], ag_r.at[n, 5], to_left)

    def pair_buffer(kind, slot):
        _, own, left, right, far, _, _, _ = kinds[kind]
        return (own, own, left, left, right, right, far, far)[slot]

    def pair_out(kind, slot):
        n, base = kinds[kind][0] - 2, kinds[kind][7]
        ref = pair_buffer(kind, slot).at[part(base, slot % 2)]
        send(ref, ref, pa_s.at[n, slot], pa_r.at[n, slot], other)

    def pair_wait(kind, slot):
        n = kinds[kind][0] - 2
        ref = pair_buffer(kind, slot).at[part((1 - row) * ROWS, slot % 2)]
        arrived(ref, pa_s.at[n, slot], pa_r.at[n, slot], other)

    for kind in ("xt", "og"):
        ring_out(kind, 0, "r")
        ring_out(kind, 1, "l")
    for kind in ("xt", "og"):
        ring_out(kind, 1, "r")
        ring_out(kind, 0, "l")

    for c in range(2):
        here = pl.ds(c * CH, CH)
        arrived(pre_in.at[here], ex_s.at[c], ex_r.at[c], other)
        arrived(back_in.at[here], ex_s.at[2 + c], ex_r.at[2 + c], other)

        def one(i, carry, c=c):
            mine = row * ROWS + c * CH + i
            pre = pre_ref[mine].astype(F32) + pre_in[c * CH + i].astype(F32)
            back = back_ref[mine].astype(F32) + back_in[c * CH + i].astype(F32)
            hidden, pre_grad = activate(pre, back)
            pg_own[mine] = pre_grad.astype(BF)
            ht_own[mine] = hidden.astype(BF).T
            return carry

        lax.fori_loop(0, CH, one, 0)
        for kind in ("pg", "ht"):
            pair_out(kind, c)
    for kind in ("pg", "ht"):
        ring_out(kind, 0, "r")
        ring_out(kind, 1, "l")
    for kind in ("pg", "ht"):
        ring_out(kind, 1, "r")
        ring_out(kind, 0, "l")
    for kind in ("xt", "og"):
        ring_wait(kind, 0)
        ring_forward(kind, "r")
        ring_wait(kind, 3)
        ring_forward(kind, "l")

    pair_wait("pg", 0)
    pair_wait("pg", 1)
    weights.wait()
    unroll = 12

    def run(i, total):
        products = []
        for j in range(unroll):
            r = i * unroll + j
            products.append(dot(pg_own[sx_h[r]], wu[sx_k[r]], NT))
        for j in range(unroll):
            r = i * unroll + j
            total = total * keep[r] + products[j]
            runs[r] = total.astype(BF)
        return total

    lax.fori_loop(0, NBLK // unroll, run, jnp.zeros((B, B), F32))
    for f in range(ROWS):
        dxp[:, f * B : (f + 1) * B] = (runs[last[f]].astype(F32) * some[f]).astype(BF)
    for d in range(1, SIDE):
        theirs = pl.ds(pl.multiple_of(((col + d) % SIDE) * 32, 32), 32)
        send(dxp.at[theirs], zin.at[d - 1], z_s.at[d - 1], z_r.at[d - 1], z_peers[d - 1])

    for kind in ("xt", "og"):
        for slot in (1, 2):
            ring_wait(kind, slot)
    for kind in ("pg", "ht"):
        ring_wait(kind, 0)
        ring_forward(kind, "r")
        pair_out(kind, 2)
        ring_wait(kind, 3)
        ring_forward(kind, "l")
        pair_out(kind, 5)
    for kind in ("pg", "ht"):
        ring_wait(kind, 1)
        pair_out(kind, 3)
        ring_wait(kind, 2)
        pair_out(kind, 4)
    for kind in ("xt", "og"):
        for slot in (4, 5):
            ring_wait(kind, slot)
    for slot in (4, 5):
        for kind in ("pg", "ht"):
            ring_wait(kind, slot)
            pair_out(kind, slot + 2)
    for kind in ("ht",):
        for slot in range(2):
            pair_wait(kind, slot)
    for slot in range(2, 8):
        for kind in ("pg", "ht"):
            pair_wait(kind, slot)

    def up_block(s):
        f, h = gu_f[s], gu_h[s]
        left = jnp.concatenate([xt_own[f], xt_l[f], xt_r[f], xt_o[f]], axis=1)
        right = jnp.concatenate([pg_own[h], pg_l[h], pg_r[h], pg_o[h]], axis=0)
        return dot(left, right, NN)

    def dn_block(s):
        f, h = gd_f[s], gd_h[s]
        left = jnp.concatenate([ht_own[h], ht_l[h], ht_r[h], ht_o[h]], axis=1)
        right = jnp.concatenate([og_own[f], og_l[f], og_r[f], og_o[f]], axis=0)
        return dot(left, right, NN)

    def up_base(d):
        return ((y + d) % SIDE) * (SIDE * SHARE) + x * SHARE

    def dn_base(d):
        return y * (SIDE * SHARE) + ((x + d) % SIDE) * SHARE

    half = SHARE // 2

    def fill(block, base, out, first, added=None):
        def body(i, carry):
            for j in range(3):
                at = first + i * 3 + j
                value = block(base + at)
                if added is not None:
                    value = value + added[i * 3 + j].astype(F32)
                out[at] = value.astype(out.dtype)
            return carry

        lax.fori_loop(0, half // 3, body, 0)

    sides = (
        (0, up_block, up_base, y_right, y_left, uf_s, ur_s, ul_s, ua_t, ub_t, ul_v, ur_v, u_acc, up_out),
        (1, dn_block, dn_base, x_right, x_left, df_s, dr_s, dl_s, da_t, db_t, dl_v, dr_v, d_acc, dn_out),
    )
    for n, block, base, to_right, to_left, f_s, r_s, l_s, a_t, b_t, l_v, r_v, acc, out in sides:
        fill(block, base(2), f_s, 0)
        send(f_s.at[pl.ds(0, half)], a_t, rs_s.at[n, 0], rs_r.at[n, 0], to_right)
        fill(block, base(2), f_s, half)
        send(f_s.at[pl.ds(half, half)], b_t, rs_s.at[n, 1], rs_r.at[n, 1], to_left)
    for n, block, base, to_right, to_left, f_s, r_s, l_s, a_t, b_t, l_v, r_v, acc, out in sides:
        fill(block, base(1), r_s, half)
        arrived(a_t, rs_s.at[n, 0], rs_r.at[n, 0], to_left)
        fill(block, base(1), r_s, 0, a_t)
        send(r_s, l_v, rs_s.at[n, 2], rs_r.at[n, 2], to_right)
        fill(block, base(3), l_s, 0)
        arrived(b_t, rs_s.at[n, 1], rs_r.at[n, 1], to_right)
        fill(block, base(3), l_s, half, b_t)
        send(l_s, r_v, rs_s.at[n, 3], rs_r.at[n, 3], to_left)
    for n, block, base, to_right, to_left, f_s, r_s, l_s, a_t, b_t, l_v, r_v, acc, out in sides:
        fill(block, base(0), acc, 0)
        fill(block, base(0), acc, half)

    for d in range(1, SIDE):
        arrived(zin.at[d - 1], z_s.at[d - 1], z_r.at[d - 1], z_peers[d - 1])
    own_rows = pl.ds(pl.multiple_of(col * 32, 32), 32)
    dx_out[...] = (
        dxp[own_rows, :].astype(F32) + zin[0].astype(F32) + zin[1].astype(F32) + zin[2].astype(F32)
    ).astype(BF)
    for n, block, base, to_right, to_left, f_s, r_s, l_s, a_t, b_t, l_v, r_v, acc, out in sides:
        arrived(l_v, rs_s.at[n, 2], rs_r.at[n, 2], to_left)
        arrived(r_v, rs_s.at[n, 3], rs_r.at[n, 3], to_right)

        def total(i, carry, acc=acc, l_v=l_v, r_v=r_v, out=out):
            out[i] = (acc[i] + l_v[i].astype(F32) + r_v[i].astype(F32)).astype(BF)
            return carry

        lax.fori_loop(0, SHARE, total, 0)
    for copy in started:
        copy.wait_send()


def backward(tables, pre, back, xt, ogb, wu):
    smem = pl.BlockSpec(memory_space=pltpu.SMEM)
    vmem = pl.BlockSpec(memory_space=pltpu.VMEM)

    def blocks(n, dtype=BF):
        return pltpu.VMEM((n, B, B), dtype)

    side = [blocks(SHARE)] * 3 + [blocks(SHARE // 2)] * 2 + [blocks(SHARE)] * 2 + [blocks(SHARE, F32)]
    dma = pltpu.SemaphoreType.DMA
    scratch = (
        [blocks(ROWS)] * 2
        + [blocks(COLS)] * 2
        + [blocks(ROWS)] * 6
        + [blocks(COLS)] * 6
        + [blocks(NBLK), blocks(NBLK), pltpu.VMEM((B, ROWS * B), BF), pltpu.VMEM((3, 32, ROWS * B), BF)]
        + side
        + side
        + [dma((4,))] * 2
        + [dma((4, 6))] * 2
        + [dma((2, 8))] * 2
        + [dma((2, 4))] * 2
        + [dma((3,))] * 2
        + [dma(())]
    )
    return pl.pallas_call(
        back_kernel,
        out_shape=[
            jax.ShapeDtypeStruct((32, ROWS * B), BF),
            jax.ShapeDtypeStruct((SHARE, B, B), BF),
            jax.ShapeDtypeStruct((SHARE, B, B), BF),
        ],
        in_specs=[smem] * 9 + [vmem] * 4 + [pl.BlockSpec(memory_space=pl.ANY)],
        out_specs=[vmem] * 3,
        scratch_shapes=scratch,
        compiler_params=pltpu.CompilerParams(
            collective_id=0, has_side_effects=True, vmem_limit_bytes=62 * 2**20
        ),
        name="backward",
    )(*tables, pre, back, xt, ogb, wu)


def shards(tokens_in, out_grad, up_weight, down_weight, up_blocks, down_blocks, owners):
    up, down, owner = up_blocks[0, 0], down_blocks[0, 0], owners[0, 0]
    slots = jnp.arange(NBLK, dtype=jnp.int32)
    at_owner = owner[None, :] == slots[:, None]
    up_owned = jnp.sum(jnp.where(at_owner, up[None, :], 0), axis=1)
    down_owned = jnp.sum(jnp.where(at_owner, down[None, :], 0), axis=1)
    rank = jnp.sum((up[None, :] < up[:, None]).astype(jnp.int32), axis=1)
    at_rank = rank[None, :] == slots[:, None]
    order = jnp.sum(jnp.where(at_rank, slots[None, :], 0), axis=1)
    ranked = jnp.sum(jnp.where(at_rank, up[None, :], 0), axis=1)
    feature = ranked // COLS
    keep = jnp.concatenate([jnp.zeros((1,), F32), (feature[1:] == feature[:-1]).astype(F32)])
    below = jnp.sum(
        (up[None, :] < (jnp.arange(ROWS, dtype=jnp.int32)[:, None] + 1) * COLS).astype(jnp.int32), axis=1
    )
    some = (below > jnp.concatenate([jnp.zeros((1,), jnp.int32), below[:-1]])).astype(F32)
    last = jnp.maximum(below - 1, 0)
    tables = (
        up_owned // COLS, up_owned % COLS, down_owned % ROWS, down_owned // ROWS,
        ranked % COLS, order, keep, last, some,
    )
    pre, back, xt, ogb = forward(
        up // COLS, up % COLS, down % ROWS, down // ROWS, tokens_in, out_grad, up_weight[0, 0], down_weight[0, 0]
    )
    input_grad, up_grad, down_grad = backward(tables, pre, back, xt, ogb, up_weight[0, 0])
    return input_grad, up_grad[None, None], down_grad[None, None]


def solution(mesh):
    placed = (
        P("dp", "row"),
        P("dp", "row"),
        P("row", "col", None, None, None),
        P("row", "col", None, None, None),
        P("row", "col", None),
        P("row", "col", None),
        P("row", "col", None),
    )
    return jax.shard_map(
        shards,
        mesh=mesh,
        in_specs=placed,
        out_specs=(
            P(("dp", "col"), "row"),
            P("row", "col", "dp", None, None),
            P("row", "col", "dp", None, None),
        ),
        check_vma=False,
    )
```

time: 412 us -> 133 us (0.32); the launches traced: 406 us -> 132 us
  matrix products: 188 us -> 0 us
  waiting for transfers between devices: 154 us -> 0 us
  Pallas kernels: 0 us -> 115 us
  local copies, waits for them, and re-layouts: 38.1 us -> 10.6 us
  between operations: 14.4 us -> 0.66 us
  other arithmetic: 10.9 us -> 6.43 us
    dot_general x15 -> x0, matrix products: 188 us -> none  [the longest x3 70.3 us: place_blocks(): jnp.einsum('tkc,kw->twc', product, table_out.astype(jnp.float32), precisi...]
    reduce_scatter x3 -> x0, waiting for transfers between devices: 146 us -> none  [the longest x1 90.6 us: shards(): lax.psum_scatter(down_term.astype(jnp.bfloat16), 'dp', scatter_dimension=...]
    pallas_call x0 -> x2, Pallas kernels: none -> 115 us  [the longest x1 95.2 us: backward(): pl.pallas_call(back_kernel, out_shape=[jax.ShapeDtypeStruct((32, ROWS * B...]
    dot_general x2 -> x0, local copies, waits for them, and re-layouts: 26.3 us -> none  [select_blocks(): jnp.einsum('tjb,kj->tkb', left3, table, preferred_element_type=jnp.float32)]
    psum x1 -> x0, waiting for transfers between devices: 8.03 us -> none  [shards(): lax.psum(pre_part.astype(jnp.bfloat16), 'row').astype(jnp.float32)]
    unnamed x7 -> x13, local copies, waits for them, and re-layouts: 4.35 us -> 10.6 us
    gather x4 -> x0, local copies, waits for them, and re-layouts: 5.08 us -> none  [the longest x1 1.4 us: shards(): up_hid_table[owner_order]]
  transfers between devices with their start and end apart: 4 -> 0, of which waited for: 3 -> 0; matrix products, arithmetic and copies ran while one was open for 21% -> 0% of each run, Pallas kernels for 0% -> 0%
where the time goes in v1:
time: 133 us; the launch traced here: 132 us
  Pallas kernels  115 us (86%)
  local copies, waits for them, and re-layouts  10.6 us (8%)
  other arithmetic  6.43 us (5%)
    pallas_call x1, Pallas kernels, backward(): pl.pallas_call(back_kernel, out_shape=[jax.ShapeDtypeStruct((32, ROWS * B...  95.2 us
    pallas_call x1, Pallas kernels, forward(): pl.pallas_call(functools.partial(forward_kernel, steps, unroll), grid_spe...  19.5 us
    unnamed x13, local copies, waits for them, and re-layouts  10.6 us

profile of v1, /device:TPU:1, one launch (start us, length us, event | category | flops | bytes accessed | tf_op | source)
XLA Modules:
  0.0 132.4 jit_solution(4816935527357094006)
XLA Ops:
  0.6 0.7 reduce.1
  1.3 0.2 convert_reduce_fusion.1
  1.5 0.6 compare_convert_fusion.refs_8_
  2.1 0.5 add_maximum_fusion.refs_7_
  2.6 0.7 reduce.2
  3.3 0.2 convert_reduce_fusion
  3.6 0.7 reduce
  4.3 0.9 select_reduce_fusion
  5.1 0.6 add_select_fusion.8
  5.7 0.6 add_select_fusion.4
  6.4 0.1 slice_compare_fusion
  6.4 0.7 add_convert_fusion.refs_6_
  7.1 0.0 copy-start.1
  7.1 1.1 copy-done.1
  8.2 0.0 copy-start.2
  8.2 1.1 copy-done.2
  9.3 19.5 %forward.1 = (bf16[48,128,128]{2,1,0:T(8,128)(2,1)S(1)}, bf16[48,128,128]{2,1,0:T(8,128)(2,1)}, bf16[24,128,128]{2,1,0:T(8,128)(2,1)S(1)}, bf16[24,128,128]{2,1,0:T(8,128)(2,1)S(1)}) custom-call(s32[288]{0:T(512)S(1)} %get-tuple-element.33.uf, s32[288]{0:T(512)S(1)} %get-tuple-element.34.uh, s32[288]{0:T(512)S(1)} %get-tuple-element.22.df, ...), custom_call_target="tpu_custom_call" | custom-call | tf_op jit(solution)/shard_map/forward/pallas_call | solution.py:86
  28.9 1.1 copy-done
  30.0 0.9 copy-done.3
  30.9 0.9 copy-done.4
  31.8 95.2 %backward.1 = (bf16[32,3072]{1,0:T(8,128)(2,1)}, bf16[18,128,128]{2,1,0:T(8,128)(2,1)}, bf16[18,128,128]{2,1,0:T(8,128)(2,1)}) custom-call(s32[288]{0:T(512)} %get-tuple-element.30.refs_0_, s32[288]{0:T(512)} %get-tuple-element.29.refs_1_, s32[288]{0:T(512)} %get-tuple-element.31.refs_2_, s32[288]{0:T(512)} %get-tuple-element.32.refs_3_, ...), custom_call_target="tpu_custom_call" | custom-call | tf_op jit(solution)/shard_map/backward/pallas_call | solution.py:388
  127.0 1.6 %copy.13 = bf16[32,3072]{1,0:T(8,128)(2,1)} copy(bf16[32,3072]{1,0:T(8,128)(2,1)} %get-tuple-element.38) | data formatting | bytes 393216
  128.6 1.9 %copy.14 = bf16[1,1,18,128,128]{4,3,2,1,0:T(8,128)(2,1)} copy(bf16[1,1,18,128,128]{4,3,2,1,0:T(8,128)(2,1)} %bitcast.9) | data formatting | bytes 1179648
  130.5 1.9 %copy.15 = bf16[1,1,18,128,128]{4,3,2,1,0:T(8,128)(2,1)} copy(bf16[1,1,18,128,128]{4,3,2,1,0:T(8,128)(2,1)} %bitcast.8) | data formatting | bytes 1179648
  (5 shorter events, 0.0 us)
Async XLA Ops:
  7.1 1.1 copy-start.1
  8.2 1.1 copy-start.2
  28.9 1.1 copy-start
  30.0 0.9 copy-start.3
  30.9 0.9 copy-start.4

commit v2 on v1

v2 whole, which is shorter than its diff:
```python
import functools

import jax
import jax.numpy as jnp
from jax import lax
from jax.experimental import pallas as pl
from jax.experimental.pallas import tpu as pltpu
from jax.sharding import PartitionSpec as P

BF = jnp.bfloat16
F32 = jnp.float32
B = 128
ROWS = 24
COLS = 48
NBLK = 288
SIDE = 4
SHARE = 18
CH = 12
PAIRS = 168
WIDE = 384
NN = (((1,), (0,)), ((), ()))
NT = (((1,), (1,)), ((), ()))
MESH = pl.DeviceIdType.MESH

root_two_pi = 0.7978845608028654
cubic_coef = 0.044715


def activate(pre_sum, back_sum):
    square = pre_sum * pre_sum
    inner_arg = root_two_pi * (pre_sum + cubic_coef * square * pre_sum)
    tanh_inner = jnp.tanh(inner_arg)
    half = 0.5 * (1.0 + tanh_inner)
    slope = half + 0.5 * pre_sum * (1.0 - tanh_inner * tanh_inner) * root_two_pi * (
        1.0 + 3.0 * cubic_coef * square
    )
    return pre_sum * half, back_sum * slope


def dot(left, right, dims):
    return lax.dot_general(left, right, dims, preferred_element_type=F32)


def prepare_kernel(up_ref, dn_ref, own_ref, out_ref):
    def iota(shape, axis):
        return lax.broadcasted_iota(jnp.int32, shape, axis)

    square = (NBLK, NBLK)
    sub, lane = iota(square, 0), iota(square, 1)
    wide = iota((NBLK, WIDE), 1)
    one, zero = jnp.float32(1), jnp.float32(0)

    def count(mask, axis):
        return jnp.sum(jnp.where(mask, one, zero), axis=axis, keepdims=True)

    def column(row):
        picked = jnp.where(sub == lane, jnp.broadcast_to(row, square).astype(F32), zero)
        return jnp.sum(picked, axis=1, keepdims=True).astype(jnp.int32)

    def pairs(e_row, e_col, split, segment, operand):
        seg_row, seg_col = segment(e_row), segment(e_col)
        same = seg_col == seg_row
        turn = count(same & (lane < sub), 1).astype(jnp.int32)
        even = (turn & 1) == 0
        turn_row = count(same & (sub < lane), 0).astype(jnp.int32)
        even_row = (turn_row & 1) == 0
        offset = count((seg_row < seg_col) & even_row, 1).astype(jnp.int32)
        place = 2 * (offset + (turn >> 1)) + (turn & 1)
        block = NBLK - iota((NBLK, 1), 0)
        value = block * 64 + operand(e_col) + jnp.where(turn >= 2, 65536, 0)
        table = jnp.sum(jnp.where(place == wide, value.astype(F32), zero), axis=0, keepdims=True)
        through = count((seg_col <= wide) & even, 0)
        here = count((seg_col == wide) & even, 0)
        last = jnp.where(here > zero, through - one, jnp.float32(PAIRS))
        return table.astype(jnp.int32), last.astype(jnp.int32)

    up_row, dn_row, owner_row = up_ref[...], dn_ref[...], own_ref[...]
    up_col, dn_col, owner_col = column(up_row), column(dn_row), column(owner_row)

    def owned(value):
        picked = jnp.where(owner_col == wide, value.astype(F32), zero)
        return jnp.sum(picked, axis=0, keepdims=True).astype(jnp.int32)

    def div(value, by):
        return (value.astype(F32) * jnp.float32(1.0 / by) + jnp.float32(0.5 / by)).astype(jnp.int32)

    def rem(value, by):
        return value - div(value, by) * by

    t0, l0 = pairs(up_row, up_col, COLS, lambda e: rem(e, COLS), lambda e: div(e, COLS))
    t1, l1 = pairs(dn_row, dn_col, ROWS, lambda e: div(e, ROWS), lambda e: rem(e, ROWS))
    t2, l2 = pairs(up_row, up_col, COLS, lambda e: div(e, COLS), lambda e: rem(e, COLS))
    rows = (
        t0, t1, t2, l0, l1, l2,
        owned(div(up_col, COLS) * 64 + rem(up_col, COLS)),
        owned(rem(dn_col, ROWS) * 64 + div(dn_col, ROWS)),
    )
    for n, value in enumerate(rows):
        out_ref[n : n + 1, :] = value


def prepare(up, down, owner):
    return pl.pallas_call(
        prepare_kernel,
        out_shape=jax.ShapeDtypeStruct((8, WIDE), jnp.int32),
        name="prepare",
    )(up, down, owner)


def main_kernel(*refs):
    tab, x_hbm, g_hbm, wu_hbm, wd_hbm = refs[:5]
    dx_out, up_out, dn_out = refs[5:8]
    (
        x_in, og_own, xt_own, wu, wd, runs,
        pre_ref, back_ref, pre_to, back_to, pre_in, back_in, pg_own, ht_own,
        xt_l, xt_r, xt_o, og_l, og_r, og_o,
        pg_l, pg_r, pg_o, ht_l, ht_r, ht_o,
        dxp, zin,
        uf_s, ur_s, ul_s, ua_t, ub_t, ul_v, ur_v, u_acc,
        df_s, dr_s, dl_s, da_t, db_t, dl_v, dr_v, d_acc,
        ex_s, ex_r, ag_s, ag_r, pa_s, pa_r, rs_s, rs_r, z_s, z_r, in_s, col_s,
    ) = refs[8:]
    def column_loads(src, dst, n):
        return [
            pltpu.make_async_copy(src.at[:, pl.ds(f * B, B)], dst.at[f], col_s.at[n, f]) for f in range(ROWS)
        ]

    loads = [
        column_loads(g_hbm, og_own, 0),
        column_loads(x_hbm, x_in, 1),
        [pltpu.make_async_copy(wu_hbm, wu.at[pl.ds(0, NBLK)], in_s.at[0])],
        [pltpu.make_async_copy(wd_hbm, wd.at[pl.ds(0, NBLK)], in_s.at[1])],
    ]

    def loaded(n):
        for load in loads[n]:
            load.wait()

    for group in loads:
        for load in group:
            load.start()
    wu[NBLK] = jnp.zeros((B, B), BF)
    wd[NBLK] = jnp.zeros((B, B), BF)
    runs[PAIRS] = jnp.zeros((B, B), BF)
    dp, row, col = lax.axis_index("dp"), lax.axis_index("row"), lax.axis_index("col")
    y, x = dp // SIDE, dp % SIDE
    other = (dp, 1 - row, col)
    x_right = (y * SIDE + (x + 1) % SIDE, row, col)
    x_left = (y * SIDE + (x + 3) % SIDE, row, col)
    y_right = (((y + 1) % SIDE) * SIDE + x, row, col)
    y_left = (((y + 3) % SIDE) * SIDE + x, row, col)
    z_peers = [(dp, row, (col + d) % SIDE) for d in range(1, SIDE)]

    barrier = pltpu.get_barrier_semaphore()
    peers = [other, x_right, x_left, y_right, y_left] + z_peers
    for peer in peers:
        pl.semaphore_signal(barrier, inc=1, device_id=peer, device_id_type=MESH)
    pl.semaphore_wait(barrier, len(peers))

    started = []

    def send(src, dst, send_sem, recv_sem, peer):
        copy = pltpu.make_async_remote_copy(
            src_ref=src, dst_ref=dst, send_sem=send_sem, recv_sem=recv_sem, device_id=peer, device_id_type=MESH
        )
        copy.start()
        started.append(copy)

    def arrived(dst, send_sem, recv_sem, peer):
        pltpu.make_async_remote_copy(
            src_ref=dst, dst_ref=dst, send_sem=send_sem, recv_sem=recv_sem, device_id=peer, device_id_type=MESH
        ).wait_recv()

    kinds = {
        "xt": (0, xt_own, xt_l, xt_r, xt_o, x_right, x_left),
        "og": (1, og_own, og_l, og_r, og_o, y_right, y_left),
        "pg": (2, pg_own, pg_l, pg_r, pg_o, x_right, x_left),
        "ht": (3, ht_own, ht_l, ht_r, ht_o, y_right, y_left),
    }

    def part(kind, c, whose=row):
        return pl.ds((whose * ROWS if kind in ("pg", "ht") else 0) + c * CH, CH)

    def ring_out(kind, c, way):
        n, own, left, right, _, to_right, to_left = kinds[kind]
        at = part(kind, c)
        if way == "r":
            send(own.at[at], left.at[at], ag_s.at[n, c], ag_r.at[n, c], to_right)
        else:
            send(own.at[at], right.at[at], ag_s.at[n, 2 + c], ag_r.at[n, 2 + c], to_left)

    def ring_wait(kind, slot):
        n, _, left, right, far, to_right, to_left = kinds[kind]
        dst = (left, left, right, right, far, far)[slot].at[part(kind, slot % 2)]
        arrived(dst, ag_s.at[n, slot], ag_r.at[n, slot], to_right)

    def ring_forward(kind, way):
        n, _, left, right, far, to_right, to_left = kinds[kind]
        if way == "r":
            at = part(kind, 0)
            send(left.at[at], far.at[at], ag_s.at[n, 4], ag_r.at[n, 4], to_right)
        else:
            at = part(kind, 1)
            send(right.at[at], far.at[at], ag_s.at[n, 5], ag_r.at[n, 5], to_left)

    def pair_buffer(kind, slot):
        _, own, left, right, far, _, _ = kinds[kind]
        return (own, own, left, left, right, right, far, far)[slot]

    def pair_out(kind, slot):
        n = kinds[kind][0] - 2
        ref = pair_buffer(kind, slot).at[part(kind, slot % 2)]
        send(ref, ref, pa_s.at[n, slot], pa_r.at[n, slot], other)

    def pair_wait(kind, slot):
        n = kinds[kind][0] - 2
        ref = pair_buffer(kind, slot).at[part(kind, slot % 2, 1 - row)]
        arrived(ref, pa_s.at[n, slot], pa_r.at[n, slot], other)

    loaded(0)
    ring_out("og", 0, "r")
    ring_out("og", 1, "l")
    ring_out("og", 1, "r")
    ring_out("og", 0, "l")
    loaded(1)
    for f in range(ROWS):
        xt_own[f] = x_in[f].T
    ring_out("xt", 0, "r")
    ring_out("xt", 1, "l")
    ring_out("xt", 1, "r")
    ring_out("xt", 0, "l")

    def products(n, left, weights, axis, count, unroll):
        def body(i, total):
            parts = []
            for j in range(unroll):
                p = i * unroll + j
                first, second = tab[n, 2 * p], tab[n, 2 * p + 1]
                lhs = jnp.concatenate([left(first & 63), left(second & 63)], axis=1)
                rhs = jnp.concatenate(
                    [weights[NBLK - ((first >> 6) & 1023)], weights[NBLK - ((second >> 6) & 1023)]], axis=axis
                )
                parts.append(((first >> 16).astype(F32), dot(lhs, rhs, NT if axis else NN)))
            for j in range(unroll):
                total = total * parts[j][0] + parts[j][1]
                runs[i * unroll + j] = total.astype(BF)
            return total

        lax.fori_loop(0, count // unroll, body, jnp.zeros((B, B), F32))

    def exchange(n, to, mine, into):
        def pick(i, carry):
            for j in range(6):
                at = i * 6 + j
                to[at] = runs[tab[3 + n, (1 - row) * ROWS + at]]
            return carry

        def own(i, carry):
            for j in range(6):
                at = i * 6 + j
                mine[at] = runs[tab[3 + n, row * ROWS + at]]
            return carry

        for c in range(2):
            lax.fori_loop(2 * c, 2 * c + 2, pick, 0)
            here = pl.ds(c * CH, CH)
            send(to.at[here], into.at[here], ex_s.at[2 * n + c], ex_r.at[2 * n + c], other)
        lax.fori_loop(0, 4, own, 0)

    loaded(2)
    products(0, lambda f: x_in[f], wu, 0, PAIRS, 12)
    exchange(0, pre_to, pre_ref, pre_in)
    for kind in ("og", "xt"):
        ring_wait(kind, 0)
        ring_forward(kind, "r")
        ring_wait(kind, 3)
        ring_forward(kind, "l")
    loaded(3)
    products(1, lambda f: og_own[f], wd, 1, PAIRS, 12)
    exchange(1, back_to, back_ref, back_in)

    for c in range(2):
        here = pl.ds(c * CH, CH)
        arrived(pre_in.at[here], ex_s.at[c], ex_r.at[c], other)
        arrived(back_in.at[here], ex_s.at[2 + c], ex_r.at[2 + c], other)

        def one(i, carry, c=c):
            mine = row * ROWS + c * CH + i
            pre = pre_ref[c * CH + i].astype(F32) + pre_in[c * CH + i].astype(F32)
            back = back_ref[c * CH + i].astype(F32) + back_in[c * CH + i].astype(F32)
            hidden, pre_grad = activate(pre, back)
            pg_own[mine] = pre_grad.astype(BF)
            ht_own[mine] = hidden.astype(BF).T
            return carry

        lax.fori_loop(0, CH, one, 0)
        for kind in ("pg", "ht"):
            pair_out(kind, c)
    for kind in ("pg", "ht"):
        ring_out(kind, 0, "r")
        ring_out(kind, 1, "l")
    for kind in ("pg", "ht"):
        ring_out(kind, 1, "r")
        ring_out(kind, 0, "l")

    pair_wait("pg", 0)
    pair_wait("pg", 1)
    products(2, lambda h: pg_own[h], wu, 1, 156, 12)
    for f in range(ROWS):
        dxp[:, f * B : (f + 1) * B] = runs[tab[5, f]]
    for d in range(1, SIDE):
        theirs = pl.ds(pl.multiple_of(((col + d) % SIDE) * 32, 32), 32)
        send(dxp.at[theirs], zin.at[d - 1], z_s.at[d - 1], z_r.at[d - 1], z_peers[d - 1])

    for kind in ("xt", "og"):
        for slot in (1, 2):
            ring_wait(kind, slot)
    for kind in ("pg", "ht"):
        ring_wait(kind, 0)
        ring_forward(kind, "r")
        pair_out(kind, 2)
        ring_wait(kind, 3)
        ring_forward(kind, "l")
        pair_out(kind, 5)
    for kind in ("pg", "ht"):
        ring_wait(kind, 1)
        pair_out(kind, 3)
        ring_wait(kind, 2)
        pair_out(kind, 4)
    for kind in ("xt", "og"):
        for slot in (4, 5):
            ring_wait(kind, slot)
    for slot in (4, 5):
        for kind in ("pg", "ht"):
            ring_wait(kind, slot)
            pair_out(kind, slot + 2)
    for kind in ("ht",):
        for slot in range(2):
            pair_wait(kind, slot)
    for slot in range(2, 8):
        for kind in ("pg", "ht"):
            pair_wait(kind, slot)

    def up_block(s):
        e = tab[6, s]
        f, h = e >> 6, e & 63
        left = jnp.concatenate([xt_own[f], xt_l[f], xt_r[f], xt_o[f]], axis=1)
        right = jnp.concatenate([pg_own[h], pg_l[h], pg_r[h], pg_o[h]], axis=0)
        return dot(left, right, NN)

    def dn_block(s):
        e = tab[7, s]
        f, h = e >> 6, e & 63
        left = jnp.concatenate([ht_own[h], ht_l[h], ht_r[h], ht_o[h]], axis=1)
        right = jnp.concatenate([og_own[f], og_l[f], og_r[f], og_o[f]], axis=0)
        return dot(left, right, NN)

    def up_base(d):
        return ((y + d) % SIDE) * (SIDE * SHARE) + x * SHARE

    def dn_base(d):
        return y * (SIDE * SHARE) + ((x + d) % SIDE) * SHARE

    half = SHARE // 2

    def fill(block, base, out, first, added=None):
        def body(i, carry):
            for j in range(9):
                at = first + i * 9 + j
                value = block(base + at)
                if added is not None:
                    value = value + added[i * 9 + j].astype(F32)
                out[at] = value.astype(out.dtype)
            return carry

        lax.fori_loop(0, half // 9, body, 0)

    sides = (
        (0, up_block, up_base, y_right, y_left, uf_s, ur_s, ul_s, ua_t, ub_t, ul_v, ur_v, u_acc, up_out),
        (1, dn_block, dn_base, x_right, x_left, df_s, dr_s, dl_s, da_t, db_t, dl_v, dr_v, d_acc, dn_out),
    )
    for n, block, base, to_right, to_left, f_s, r_s, l_s, a_t, b_t, l_v, r_v, acc, out in sides:
        fill(block, base(2), f_s, 0)
        send(f_s.at[pl.ds(0, half)], a_t, rs_s.at[n, 0], rs_r.at[n, 0], to_right)
        fill(block, base(2), f_s, half)
        send(f_s.at[pl.ds(half, half)], b_t, rs_s.at[n, 1], rs_r.at[n, 1], to_left)
    for n, block, base, to_right, to_left, f_s, r_s, l_s, a_t, b_t, l_v, r_v, acc, out in sides:
        fill(block, base(1), r_s, half)
        arrived(a_t, rs_s.at[n, 0], rs_r.at[n, 0], to_left)
        fill(block, base(1), r_s, 0, a_t)
        send(r_s, l_v, rs_s.at[n, 2], rs_r.at[n, 2], to_right)
        fill(block, base(3), l_s, 0)
        arrived(b_t, rs_s.at[n, 1], rs_r.at[n, 1], to_right)
        fill(block, base(3), l_s, half, b_t)
        send(l_s, r_v, rs_s.at[n, 3], rs_r.at[n, 3], to_left)
    for n, block, base, to_right, to_left, f_s, r_s, l_s, a_t, b_t, l_v, r_v, acc, out in sides:
        fill(block, base(0), acc, 0)
        fill(block, base(0), acc, half)

    for d in range(1, SIDE):
        arrived(zin.at[d - 1], z_s.at[d - 1], z_r.at[d - 1], z_peers[d - 1])
    own_rows = pl.ds(pl.multiple_of(col * 32, 32), 32)
    dx_out[...] = (
        dxp[own_rows, :].astype(F32) + zin[0].astype(F32) + zin[1].astype(F32) + zin[2].astype(F32)
    ).astype(BF)
    for n, block, base, to_right, to_left, f_s, r_s, l_s, a_t, b_t, l_v, r_v, acc, out in sides:
        arrived(l_v, rs_s.at[n, 2], rs_r.at[n, 2], to_left)
        arrived(r_v, rs_s.at[n, 3], rs_r.at[n, 3], to_right)

        def total(i, carry, acc=acc, l_v=l_v, r_v=r_v, out=out):
            out[i] = (acc[i] + l_v[i].astype(F32) + r_v[i].astype(F32)).astype(BF)
            return carry

        lax.fori_loop(0, SHARE, total, 0)
    for copy in started:
        copy.wait_send()


def main(table, x, g, wu, wd):
    vmem = pl.BlockSpec(memory_space=pltpu.VMEM)
    far = pl.BlockSpec(memory_space=pl.ANY)

    def blocks(n, dtype=BF):
        return pltpu.VMEM((n, B, B), dtype)

    tokens = pltpu.VMEM((B, ROWS * B), BF)
    side = [blocks(SHARE)] * 3 + [blocks(SHARE // 2)] * 2 + [blocks(SHARE)] * 2 + [blocks(SHARE, F32)]
    dma = pltpu.SemaphoreType.DMA
    scratch = (
        [blocks(ROWS)] * 3 + [blocks(NBLK + 1), blocks(NBLK + 1), blocks(PAIRS + 1)]
        + [blocks(ROWS)] * 6
        + [blocks(COLS)] * 2
        + [blocks(ROWS)] * 3
        + [blocks(ROWS)] * 3
        + [blocks(COLS)] * 6
        + [tokens, pltpu.VMEM((3, 32, ROWS * B), BF)]
        + side
        + side
        + [dma((4,))] * 2
        + [dma((4, 6))] * 2
        + [dma((2, 8))] * 2
        + [dma((2, 4))] * 2
        + [dma((3,))] * 2
        + [dma((2,)), dma((2, ROWS))]
    )
    return pl.pallas_call(
        main_kernel,
        out_shape=[
            jax.ShapeDtypeStruct((32, ROWS * B), BF),
            jax.ShapeDtypeStruct((SHARE, B, B), BF),
            jax.ShapeDtypeStruct((SHARE, B, B), BF),
        ],
        in_specs=[pl.BlockSpec(memory_space=pltpu.SMEM)] + [far] * 4,
        out_specs=[vmem] * 3,
        scratch_shapes=scratch,
        compiler_params=pltpu.CompilerParams(
            collective_id=0, has_side_effects=True, vmem_limit_bytes=62 * 2**20
        ),
        name="backward",
    )(table, x, g, wu, wd)


def shards(tokens_in, out_grad, up_weight, down_weight, up_blocks, down_blocks, owners):
    table = prepare(up_blocks[0], down_blocks[0], owners[0])
    input_grad, up_grad, down_grad = main(table, tokens_in, out_grad, up_weight[0, 0], down_weight[0, 0])
    return input_grad, up_grad[None, None], down_grad[None, None]


def solution(mesh):
    placed = (
        P("dp", "row"),
        P("dp", "row"),
        P("row", "col", None, None, None),
        P("row", "col", None, None, None),
        P("row", "col", None),
        P("row", "col", None),
        P("row", "col", None),
    )
    return jax.shard_map(
        shards,
        mesh=mesh,
        in_specs=placed,
        out_specs=(
            P(("dp", "col"), "row"),
            P("row", "col", "dp", None, None),
            P("row", "col", "dp", None, None),
        ),
        check_vma=False,
    )
```

time: 133 us -> 105 us (0.79)
  Pallas kernels: 115 us -> 98.7 us
  other arithmetic: 6.43 us -> 0 us
  local copies, waits for them, and re-layouts: 10.6 us -> 5.47 us
    pallas_call x2, Pallas kernels: 115 us -> 98.7 us  [the longest x1 96 us: main(): pl.pallas_call(main_kernel, out_shape=[jax.ShapeDtypeStruct((32, ROWS * B...]
    unnamed x13 -> x3, local copies, waits for them, and re-layouts: 10.6 us -> 5.47 us
    unnamed x3 -> x0, other arithmetic: 2.1 us -> none
where the time goes in v2:
time: 105 us
  Pallas kernels  98.7 us (94%)
  local copies, waits for them, and re-layouts  5.47 us (5%)
    pallas_call x1, Pallas kernels, main(): pl.pallas_call(main_kernel, out_shape=[jax.ShapeDtypeStruct((32, ROWS * B...  96 us
    unnamed x3, local copies, waits for them, and re-layouts  5.47 us
    pallas_call x1, Pallas kernels, prepare(): pl.pallas_call(prepare_kernel, out_shape=jax.ShapeDtypeStruct((8, WIDE),...  2.76 us

profile of v2, /device:TPU:1, one launch (start us, length us, event | category | flops | bytes accessed | tf_op | source)
XLA Modules:
  0.0 104.9 jit_solution(15915597618892270877)
XLA Ops:
  0.6 2.8 %prepare.1.refs_0_ = s32[8,384]{1,0:T(8,128)} custom-call(s32[1,288]{1,0:T(1,128)} %bitcast.11, s32[1,288]{1,0:T(1,128)} %bitcast.12, s32[1,288]{1,0:T(1,128)} %bitcast.13), custom_call_target="tpu_custom_call" | custom-call | tf_op jit(solution)/shard_map/prepare/pallas_call | solution.py:103
  3.4 96.0 %backward.1 = (bf16[32,3072]{1,0:T(8,128)(2,1)}, bf16[18,128,128]{2,1,0:T(8,128)(2,1)}, bf16[18,128,128]{2,1,0:T(8,128)(2,1)}) custom-call(s32[8,384]{1,0:T(8,128)} %prepare.1.refs_0_, bf16[128,3072]{1,0:T(8,128)(2,1)} %refs_1_.1, bf16[128,3072]{1,0:T(8,128)(2,1)} %refs_2_.1, bf16[288,128,128]{2,1,0:T(8,128)(2,1)} %bitcast.7, bf16[288,128,128]{2,1,0:T(8,128)(2,1)} %bitcast.8), custom_call_target="tpu_custom_call" | custom-call | tf_op jit(solution)/shard_map/backward/pallas_call | solution.py:446
  99.4 1.6 %copy.13 = bf16[32,3072]{1,0:T(8,128)(2,1)} copy(bf16[32,3072]{1,0:T(8,128)(2,1)} %get-tuple-element.12) | data formatting | bytes 393216
  101.0 1.9 %copy.14 = bf16[1,1,18,128,128]{4,3,2,1,0:T(8,128)(2,1)} copy(bf16[1,1,18,128,128]{4,3,2,1,0:T(8,128)(2,1)} %bitcast.10) | data formatting | bytes 1179648
  102.9 1.9 %copy.15 = bf16[1,1,18,128,128]{4,3,2,1,0:T(8,128)(2,1)} copy(bf16[1,1,18,128,128]{4,3,2,1,0:T(8,128)(2,1)} %bitcast.9) | data formatting | bytes 1179648

commit v3 on v2

--- a/solution.py
+++ b/solution.py
@@ -120,28 +120,6 @@
         df_s, dr_s, dl_s, da_t, db_t, dl_v, dr_v, d_acc,
         ex_s, ex_r, ag_s, ag_r, pa_s, pa_r, rs_s, rs_r, z_s, z_r, in_s, col_s,
     ) = refs[8:]
-    def column_loads(src, dst, n):
-        return [
-            pltpu.make_async_copy(src.at[:, pl.ds(f * B, B)], dst.at[f], col_s.at[n, f]) for f in range(ROWS)
-        ]
-
-    loads = [
-        column_loads(g_hbm, og_own, 0),
-        column_loads(x_hbm, x_in, 1),
-        [pltpu.make_async_copy(wu_hbm, wu.at[pl.ds(0, NBLK)], in_s.at[0])],
-        [pltpu.make_async_copy(wd_hbm, wd.at[pl.ds(0, NBLK)], in_s.at[1])],
-    ]
-
-    def loaded(n):
-        for load in loads[n]:
-            load.wait()
-
-    for group in loads:
-        for load in group:
-            load.start()
-    wu[NBLK] = jnp.zeros((B, B), BF)
-    wd[NBLK] = jnp.zeros((B, B), BF)
-    runs[PAIRS] = jnp.zeros((B, B), BF)
     dp, row, col = lax.axis_index("dp"), lax.axis_index("row"), lax.axis_index("col")
     y, x = dp // SIDE, dp % SIDE
     other = (dp, 1 - row, col)
@@ -155,7 +133,29 @@
     peers = [other, x_right, x_left, y_right, y_left] + z_peers
     for peer in peers:
         pl.semaphore_signal(barrier, inc=1, device_id=peer, device_id_type=MESH)
-    pl.semaphore_wait(barrier, len(peers))
+
+    def column_loads(src, dst, n):
+        return [
+            pltpu.make_async_copy(src.at[:, pl.ds(f * B, B)], dst.at[f], col_s.at[n, f]) for f in range(ROWS)
+        ]
+
+    loads = [
+        column_loads(g_hbm, og_own, 0),
+        column_loads(x_hbm, x_in, 1),
+        [pltpu.make_async_copy(wu_hbm, wu.at[pl.ds(0, NBLK)], in_s.at[0])],
+        [pltpu.make_async_copy(wd_hbm, wd.at[pl.ds(0, NBLK)], in_s.at[1])],
+    ]
+
+    def loaded(n):
+        for load in loads[n]:
+            load.wait()
+
+    for group in loads:
+        for load in group:
+            load.start()
+    wu[NBLK] = jnp.zeros((B, B), BF)
+    wd[NBLK] = jnp.zeros((B, B), BF)
+    runs[PAIRS] = jnp.zeros((B, B), BF)
 
     started = []
 
@@ -189,46 +189,39 @@
         else:
             send(own.at[at], right.at[at], ag_s.at[n, 2 + c], ag_r.at[n, 2 + c], to_left)
 
+    def spot(kind, slot, whose=row):
+        _, own, left, right, far, _, _ = kinds[kind]
+        buffer = (own, own, left, left, right, right, far, far, far, far)[slot]
+        if slot < 6:
+            return buffer.at[part(kind, slot % 2, whose)]
+        base = whose * ROWS if kind in ("pg", "ht") else 0
+        return buffer.at[pl.ds(base + (slot - 6) * (CH // 2), CH // 2)]
+
     def ring_wait(kind, slot):
-        n, _, left, right, far, to_right, to_left = kinds[kind]
-        dst = (left, left, right, right, far, far)[slot].at[part(kind, slot % 2)]
-        arrived(dst, ag_s.at[n, slot], ag_r.at[n, slot], to_right)
+        n, to_right = kinds[kind][0], kinds[kind][5]
+        arrived(spot(kind, slot + 2), ag_s.at[n, slot], ag_r.at[n, slot], to_right)
 
     def ring_forward(kind, way):
         n, _, left, right, far, to_right, to_left = kinds[kind]
-        if way == "r":
-            at = part(kind, 0)
-            send(left.at[at], far.at[at], ag_s.at[n, 4], ag_r.at[n, 4], to_right)
-        else:
-            at = part(kind, 1)
-            send(right.at[at], far.at[at], ag_s.at[n, 5], ag_r.at[n, 5], to_left)
-
-    def pair_buffer(kind, slot):
-        _, own, left, right, far, _, _ = kinds[kind]
-        return (own, own, left, left, right, right, far, far)[slot]
+        base = row * ROWS if kind in ("pg", "ht") else 0
+        source, first, peer = (left, 4, to_right) if way == "r" else (right, 6, to_left)
+        for slot in (first, first + 1):
+            at = pl.ds(base + (slot - 4) * (CH // 2), CH // 2)
+            send(source.at[at], far.at[at], ag_s.at[n, slot], ag_r.at[n, slot], peer)
 
     def pair_out(kind, slot):
         n = kinds[kind][0] - 2
-        ref = pair_buffer(kind, slot).at[part(kind, slot % 2)]
+        ref = spot(kind, slot)
         send(ref, ref, pa_s.at[n, slot], pa_r.at[n, slot], other)
 
     def pair_wait(kind, slot):
         n = kinds[kind][0] - 2
-        ref = pair_buffer(kind, slot).at[part(kind, slot % 2, 1 - row)]
+        ref = spot(kind, slot, 1 - row)
         arrived(ref, pa_s.at[n, slot], pa_r.at[n, slot], other)
 
-    loaded(0)
-    ring_out("og", 0, "r")
-    ring_out("og", 1, "l")
-    ring_out("og", 1, "r")
-    ring_out("og", 0, "l")
     loaded(1)
     for f in range(ROWS):
         xt_own[f] = x_in[f].T
-    ring_out("xt", 0, "r")
-    ring_out("xt", 1, "l")
-    ring_out("xt", 1, "r")
-    ring_out("xt", 0, "l")
 
     def products(n, left, weights, axis, count, unroll):
         def body(i, total):
@@ -269,15 +262,23 @@
 
     loaded(2)
     products(0, lambda f: x_in[f], wu, 0, PAIRS, 12)
+    loaded(0)
+    pl.semaphore_wait(barrier, len(peers))
+    for kind in ("og", "xt"):
+        ring_out(kind, 0, "r")
+        ring_out(kind, 1, "l")
+    for kind in ("og", "xt"):
+        ring_out(kind, 1, "r")
+        ring_out(kind, 0, "l")
     exchange(0, pre_to, pre_ref, pre_in)
+    loaded(3)
+    products(1, lambda f: og_own[f], wd, 1, PAIRS, 12)
+    exchange(1, back_to, back_ref, back_in)
     for kind in ("og", "xt"):
         ring_wait(kind, 0)
         ring_forward(kind, "r")
         ring_wait(kind, 3)
         ring_forward(kind, "l")
-    loaded(3)
-    products(1, lambda f: og_own[f], wd, 1, PAIRS, 12)
-    exchange(1, back_to, back_ref, back_in)
 
     for c in range(2):
         here = pl.ds(c * CH, CH)
@@ -295,10 +296,8 @@
 
         lax.fori_loop(0, CH, one, 0)
         for kind in ("pg", "ht"):
+            ring_out(kind, c, "rl"[c])
             pair_out(kind, c)
-    for kind in ("pg", "ht"):
-        ring_out(kind, 0, "r")
-        ring_out(kind, 1, "l")
     for kind in ("pg", "ht"):
         ring_out(kind, 1, "r")
         ring_out(kind, 0, "l")
@@ -328,16 +327,16 @@
         ring_wait(kind, 2)
         pair_out(kind, 4)
     for kind in ("xt", "og"):
-        for slot in (4, 5):
+        for slot in (4, 5, 6, 7):
             ring_wait(kind, slot)
-    for slot in (4, 5):
+    for slot in (4, 6, 5, 7):
         for kind in ("pg", "ht"):
             ring_wait(kind, slot)
             pair_out(kind, slot + 2)
     for kind in ("ht",):
         for slot in range(2):
             pair_wait(kind, slot)
-    for slot in range(2, 8):
+    for slot in range(2, 10):
         for kind in ("pg", "ht"):
             pair_wait(kind, slot)
 
@@ -362,6 +361,7 @@
         return y * (SIDE * SHARE) + ((x + d) % SIDE) * SHARE
 
     half = SHARE // 2
+    early, late = pl.ds(0, half), pl.ds(half, half)
 
     def fill(block, base, out, first, added=None):
         def body(i, carry):
@@ -381,18 +381,21 @@
     )
     for n, block, base, to_right, to_left, f_s, r_s, l_s, a_t, b_t, l_v, r_v, acc, out in sides:
         fill(block, base(2), f_s, 0)
-        send(f_s.at[pl.ds(0, half)], a_t, rs_s.at[n, 0], rs_r.at[n, 0], to_right)
+        send(f_s.at[early], a_t, rs_s.at[n, 0], rs_r.at[n, 0], to_right)
         fill(block, base(2), f_s, half)
-        send(f_s.at[pl.ds(half, half)], b_t, rs_s.at[n, 1], rs_r.at[n, 1], to_left)
+        send(f_s.at[late], b_t, rs_s.at[n, 1], rs_r.at[n, 1], to_left)
     for n, block, base, to_right, to_left, f_s, r_s, l_s, a_t, b_t, l_v, r_v, acc, out in sides:
         fill(block, base(1), r_s, half)
+        send(r_s.at[late], l_v.at[late], rs_s.at[n, 2], rs_r.at[n, 2], to_right)
+        fill(block, base(3), l_s, 0)
+        send(l_s.at[early], r_v.at[early], rs_s.at[n, 3], rs_r.at[n, 3], to_left)
+    for n, block, base, to_right, to_left, f_s, r_s, l_s, a_t, b_t, l_v, r_v, acc, out in sides:
         arrived(a_t, rs_s.at[n, 0], rs_r.at[n, 0], to_left)
         fill(block, base(1), r_s, 0, a_t)
-        send(r_s, l_v, rs_s.at[n, 2], rs_r.at[n, 2], to_right)
-        fill(block, base(3), l_s, 0)
+        send(r_s.at[early], l_v.at[early], rs_s.at[n, 4], rs_r.at[n, 4], to_right)
         arrived(b_t, rs_s.at[n, 1], rs_r.at[n, 1], to_right)
         fill(block, base(3), l_s, half, b_t)
-        send(l_s, r_v, rs_s.at[n, 3], rs_r.at[n, 3], to_left)
+        send(l_s.at[late], r_v.at[late], rs_s.at[n, 5], rs_r.at[n, 5], to_left)
     for n, block, base, to_right, to_left, f_s, r_s, l_s, a_t, b_t, l_v, r_v, acc, out in sides:
         fill(block, base(0), acc, 0)
         fill(block, base(0), acc, half)
@@ -404,8 +407,10 @@
         dxp[own_rows, :].astype(F32) + zin[0].astype(F32) + zin[1].astype(F32) + zin[2].astype(F32)
     ).astype(BF)
     for n, block, base, to_right, to_left, f_s, r_s, l_s, a_t, b_t, l_v, r_v, acc, out in sides:
-        arrived(l_v, rs_s.at[n, 2], rs_r.at[n, 2], to_left)
-        arrived(r_v, rs_s.at[n, 3], rs_r.at[n, 3], to_right)
+        arrived(l_v.at[late], rs_s.at[n, 2], rs_r.at[n, 2], to_left)
+        arrived(r_v.at[early], rs_s.at[n, 3], rs_r.at[n, 3], to_right)
+        arrived(l_v.at[early], rs_s.at[n, 4], rs_r.at[n, 4], to_left)
+        arrived(r_v.at[late], rs_s.at[n, 5], rs_r.at[n, 5], to_right)
 
         def total(i, carry, acc=acc, l_v=l_v, r_v=r_v, out=out):
             out[i] = (acc[i] + l_v[i].astype(F32) + r_v[i].astype(F32)).astype(BF)
@@ -437,9 +442,9 @@
         + side
         + side
         + [dma((4,))] * 2
-        + [dma((4, 6))] * 2
-        + [dma((2, 8))] * 2
-        + [dma((2, 4))] * 2
+        + [dma((4, 8))] * 2
+        + [dma((2, 10))] * 2
+        + [dma((2, 6))] * 2
         + [dma((3,))] * 2
         + [dma((2,)), dma((2, ROWS))]
     )
@@ -460,9 +465,33 @@
     )(table, x, g, wu, wd)
 
 
+def results_kernel(*refs):
+    count = len(refs) // 2
+    sems = refs[-1]
+    copies = [pltpu.make_async_copy(refs[n], refs[count + n], sems.at[n]) for n in range(count)]
+    for copy in copies:
+        copy.start()
+    for copy in copies:
+        copy.wait()
+
+
+def results(*values):
+    far = pl.BlockSpec(memory_space=pl.ANY)
+    return pl.pallas_call(
+        results_kernel,
+        out_shape=[jax.ShapeDtypeStruct(value.shape, value.dtype) for value in values],
+        in_specs=[far] * len(values),
+        out_specs=[far] * len(values),
+        scratch_shapes=[pltpu.SemaphoreType.DMA((len(values),))],
+        name="results",
+    )(*values)
+
+
 def shards(tokens_in, out_grad, up_weight, down_weight, up_blocks, down_blocks, owners):
     table = prepare(up_blocks[0], down_blocks[0], owners[0])
-    input_grad, up_grad, down_grad = main(table, tokens_in, out_grad, up_weight[0, 0], down_weight[0, 0])
+    input_grad, up_grad, down_grad = results(
+        *main(table, tokens_in, out_grad, up_weight[0, 0], down_weight[0, 0])
+    )
     return input_grad, up_grad[None, None], down_grad[None, None]
 
 

time: 105 us -> 143 us (1.36)
  Pallas kernels: 98.7 us -> 142 us
  local copies, waits for them, and re-layouts: 5.47 us -> 0 us
    pallas_call x0 -> x1, Pallas kernels: none -> 42.8 us  [results(): pl.pallas_call(results_kernel, out_shape=[jax.ShapeDtypeStruct(value.shap...]
    unnamed x3 -> x0, local copies, waits for them, and re-layouts: 5.47 us -> none
where the time goes in v3:
time: 143 us
  Pallas kernels  142 us (99%)
    pallas_call x1, Pallas kernels, main(): pl.pallas_call(main_kernel, out_shape=[jax.ShapeDtypeStruct((32, ROWS * B...  96.8 us
    pallas_call x1, Pallas kernels, results(): pl.pallas_call(results_kernel, out_shape=[jax.ShapeDtypeStruct(value.shap...  42.8 us

profile of v3, /device:TPU:1, one launch (start us, length us, event | category | flops | bytes accessed | tf_op | source)
XLA Modules:
  0.0 143.0 jit_solution(5658348199026474991)
XLA Ops:
  0.6 2.8 %prepare.1.refs_0_ = s32[8,384]{1,0:T(8,128)} custom-call(s32[1,288]{1,0:T(1,128)} %bitcast.9, s32[1,288]{1,0:T(1,128)} %bitcast.10, s32[1,288]{1,0:T(1,128)} %bitcast.11), custom_call_target="tpu_custom_call" | custom-call | tf_op jit(solution)/shard_map/prepare/pallas_call | solution.py:103
  3.4 96.8 %backward.1 = (bf16[32,3072]{1,0:T(8,128)(2,1)}, bf16[18,128,128]{2,1,0:T(8,128)(2,1)}, bf16[18,128,128]{2,1,0:T(8,128)(2,1)}) custom-call(s32[8,384]{1,0:T(8,128)} %prepare.1.refs_0_, bf16[128,3072]{1,0:T(8,128)(2,1)} %refs_1_.1, bf16[128,3072]{1,0:T(8,128)(2,1)} %refs_2_.1, bf16[288,128,128]{2,1,0:T(8,128)(2,1)} %bitcast.7, bf16[288,128,128]{2,1,0:T(8,128)(2,1)} %bitcast.8), custom_call_target="tpu_custom_call" | custom-call | tf_op jit(solution)/shard_map/backward/pallas_call | solution.py:451
  100.2 42.8 %results.1 = (bf16[32,3072]{1,0:T(8,128)(2,1)}, bf16[18,128,128]{2,1,0:T(8,128)(2,1)}, bf16[18,128,128]{2,1,0:T(8,128)(2,1)}) custom-call(bf16[32,3072]{1,0:T(8,128)(2,1)} %get-tuple-element.9.refs_0_, bf16[18,128,128]{2,1,0:T(8,128)(2,1)} %get-tuple-element.10.refs_1_, bf16[18,128,128]{2,1,0:T(8,128)(2,1)} %get-tuple-element.11.refs_2_), custom_call_target="tpu_custom_call" | custom-call | tf_op jit(solution)/shard_map/results/pallas_call | solution.py:480

commit v4 on v3

--- a/solution.py
+++ b/solution.py
@@ -118,7 +118,7 @@
         dxp, zin,
         uf_s, ur_s, ul_s, ua_t, ub_t, ul_v, ur_v, u_acc,
         df_s, dr_s, dl_s, da_t, db_t, dl_v, dr_v, d_acc,
-        ex_s, ex_r, ag_s, ag_r, pa_s, pa_r, rs_s, rs_r, z_s, z_r, in_s, col_s,
+        ex_s, ex_r, ag_s, ag_r, pa_s, pa_r, rs_s, rs_r, z_s, z_r, in_s, col_s, to_s, to_r, sh_s, sh_r,
     ) = refs[8:]
     dp, row, col = lax.axis_index("dp"), lax.axis_index("row"), lax.axis_index("col")
     y, x = dp // SIDE, dp % SIDE
@@ -172,18 +172,61 @@
         ).wait_recv()
 
     kinds = {
-        "xt": (0, xt_own, xt_l, xt_r, xt_o, x_right, x_left),
-        "og": (1, og_own, og_l, og_r, og_o, y_right, y_left),
-        "pg": (2, pg_own, pg_l, pg_r, pg_o, x_right, x_left),
-        "ht": (3, ht_own, ht_l, ht_r, ht_o, y_right, y_left),
+        "pg": (0, pg_own, pg_l, pg_r, pg_o, x_right, x_left),
+        "ht": (1, ht_own, ht_l, ht_r, ht_o, y_right, y_left),
     }
 
-    def part(kind, c, whose=row):
-        return pl.ds((whose * ROWS if kind in ("pg", "ht") else 0) + c * CH, CH)
+    token_kinds = (
+        (0, xt_own, (xt_l, xt_r, xt_o), x_right, x_left),
+        (1, og_own, (og_l, og_r, og_o), y_right, y_left),
+    )
+    z_right, z_left = (dp, row, (col + 1) % SIDE), (dp, row, (col + 3) % SIDE)
+    first, second = pl.ds(0, 4), pl.ds(4, 4)
+
+    def share(step, offset=0, count=4):
+        return pl.ds(8 + 4 * ((col + step) % SIDE) + offset, count)
+
+    token_spots = (
+        (0, share(0), share(0)), (0, first, first), (0, second, second),
+        (1, share(0), share(0)), (1, first, first), (1, second, second),
+        (2, share(0, 0, 2), 0), (2, first, 0), (2, share(0, 2, 2), 1), (2, second, 1),
+    )
+
+    def token_send(kind, slot):
+        n, own, into, to_right, to_left = kind
+        buffer, at, source = token_spots[slot]
+        src = own if slot < 6 else into[source]
+        peer = to_right if slot in (0, 1, 2, 6, 7) else to_left
+        send(src.at[at], into[buffer].at[at], to_s.at[n, slot], to_r.at[n, slot], peer)
+
+    def token_wait(kind, slot):
+        n, _, into, to_right, _ = kind
+        buffer, at, _ = token_spots[slot]
+        arrived(into[buffer].at[at], to_s.at[n, slot], to_r.at[n, slot], to_right)
+
+    def share_send(kind, source):
+        n, _, into, _, _ = kind
+        ref = into[source].at[share(0)]
+        send(ref, ref, sh_s.at[n, source, 0], sh_r.at[n, source, 0], z_right)
+        send(ref, ref, sh_s.at[n, source, 1], sh_r.at[n, source, 1], z_left)
+
+    def share_wait(kind, source, way):
+        n, _, into, _, _ = kind
+        ref = into[source].at[share((3, 1, 2)[way])]
+        arrived(ref, sh_s.at[n, source, way], sh_r.at[n, source, way], z_right)
+
+    def share_forward(kind, source):
+        n, _, into, _, _ = kind
+        share_wait(kind, source, n)
+        ref = into[source].at[share((3, 1)[n])]
+        send(ref, ref, sh_s.at[n, source, 2], sh_r.at[n, source, 2], (z_right, z_left)[n])
+
+    def part(c, whose=row):
+        return pl.ds(whose * ROWS + c * CH, CH)
 
     def ring_out(kind, c, way):
         n, own, left, right, _, to_right, to_left = kinds[kind]
-        at = part(kind, c)
+        at = part(c)
         if way == "r":
             send(own.at[at], left.at[at], ag_s.at[n, c], ag_r.at[n, c], to_right)
         else:
@@ -193,9 +236,8 @@
         _, own, left, right, far, _, _ = kinds[kind]
         buffer = (own, own, left, left, right, right, far, far, far, far)[slot]
         if slot < 6:
-            return buffer.at[part(kind, slot % 2, whose)]
-        base = whose * ROWS if kind in ("pg", "ht") else 0
-        return buffer.at[pl.ds(base + (slot - 6) * (CH // 2), CH // 2)]
+            return buffer.at[part(slot % 2, whose)]
+        return buffer.at[pl.ds(whose * ROWS + (slot - 6) * (CH // 2), CH // 2)]
 
     def ring_wait(kind, slot):
         n, to_right = kinds[kind][0], kinds[kind][5]
@@ -203,19 +245,19 @@
 
     def ring_forward(kind, way):
         n, _, left, right, far, to_right, to_left = kinds[kind]
-        base = row * ROWS if kind in ("pg", "ht") else 0
+        base = row * ROWS
         source, first, peer = (left, 4, to_right) if way == "r" else (right, 6, to_left)
         for slot in (first, first + 1):
             at = pl.ds(base + (slot - 4) * (CH // 2), CH // 2)
             send(source.at[at], far.at[at], ag_s.at[n, slot], ag_r.at[n, slot], peer)
 
     def pair_out(kind, slot):
-        n = kinds[kind][0] - 2
+        n = kinds[kind][0]
         ref = spot(kind, slot)
         send(ref, ref, pa_s.at[n, slot], pa_r.at[n, slot], other)
 
     def pair_wait(kind, slot):
-        n = kinds[kind][0] - 2
+        n = kinds[kind][0]
         ref = spot(kind, slot, 1 - row)
         arrived(ref, pa_s.at[n, slot], pa_r.at[n, slot], other)
 
@@ -264,21 +306,22 @@
     products(0, lambda f: x_in[f], wu, 0, PAIRS, 12)
     loaded(0)
     pl.semaphore_wait(barrier, len(peers))
-    for kind in ("og", "xt"):
-        ring_out(kind, 0, "r")
-        ring_out(kind, 1, "l")
-    for kind in ("og", "xt"):
-        ring_out(kind, 1, "r")
-        ring_out(kind, 0, "l")
+    for slots in ((0, 3), (1, 5), (2, 4)):
+        for kind in token_kinds:
+            for slot in slots:
+                token_send(kind, slot)
     exchange(0, pre_to, pre_ref, pre_in)
     loaded(3)
     products(1, lambda f: og_own[f], wd, 1, PAIRS, 12)
     exchange(1, back_to, back_ref, back_in)
-    for kind in ("og", "xt"):
-        ring_wait(kind, 0)
-        ring_forward(kind, "r")
-        ring_wait(kind, 3)
-        ring_forward(kind, "l")
+    for kind in token_kinds:
+        for slot, source, forward in ((0, 0, 6), (3, 1, 8)):
+            token_wait(kind, slot)
+            share_send(kind, source)
+            token_send(kind, forward)
+        for slot, forward in ((1, 7), (5, 9)):
+            token_wait(kind, slot)
+            token_send(kind, forward)
 
     for c in range(2):
         here = pl.ds(c * CH, CH)
@@ -302,6 +345,13 @@
         ring_out(kind, 1, "r")
         ring_out(kind, 0, "l")
 
+    for kind in token_kinds:
+        token_wait(kind, 6)
+        token_wait(kind, 8)
+        share_send(kind, 2)
+        share_forward(kind, 0)
+        share_forward(kind, 1)
+
     pair_wait("pg", 0)
     pair_wait("pg", 1)
     products(2, lambda h: pg_own[h], wu, 1, 156, 12)
@@ -311,9 +361,8 @@
         theirs = pl.ds(pl.multiple_of(((col + d) % SIDE) * 32, 32), 32)
         send(dxp.at[theirs], zin.at[d - 1], z_s.at[d - 1], z_r.at[d - 1], z_peers[d - 1])
 
-    for kind in ("xt", "og"):
-        for slot in (1, 2):
-            ring_wait(kind, slot)
+    for kind in token_kinds:
+        share_forward(kind, 2)
     for kind in ("pg", "ht"):
         ring_wait(kind, 0)
         ring_forward(kind, "r")
@@ -326,9 +375,12 @@
         pair_out(kind, 3)
         ring_wait(kind, 2)
         pair_out(kind, 4)
-    for kind in ("xt", "og"):
-        for slot in (4, 5, 6, 7):
-            ring_wait(kind, slot)
+    for kind in token_kinds:
+        for slot in (2, 4, 7, 9):
+            token_wait(kind, slot)
+        for source in range(3):
+            share_wait(kind, source, 1 - kind[0])
+            share_wait(kind, source, 2)
     for slot in (4, 6, 5, 7):
         for kind in ("pg", "ht"):
             ring_wait(kind, slot)
@@ -442,11 +494,13 @@
         + side
         + side
         + [dma((4,))] * 2
-        + [dma((4, 8))] * 2
+        + [dma((2, 8))] * 2
         + [dma((2, 10))] * 2
         + [dma((2, 6))] * 2
         + [dma((3,))] * 2
         + [dma((2,)), dma((2, ROWS))]
+        + [dma((2, 10))] * 2
+        + [dma((2, 3, 3))] * 2
     )
     return pl.pallas_call(
         main_kernel,
@@ -467,22 +521,17 @@
 
 def results_kernel(*refs):
     count = len(refs) // 2
-    sems = refs[-1]
-    copies = [pltpu.make_async_copy(refs[n], refs[count + n], sems.at[n]) for n in range(count)]
-    for copy in copies:
-        copy.start()
-    for copy in copies:
-        copy.wait()
+    for n in range(count):
+        refs[count + n][...] = refs[n][...]
 
 
 def results(*values):
-    far = pl.BlockSpec(memory_space=pl.ANY)
+    vmem = pl.BlockSpec(memory_space=pltpu.VMEM)
     return pl.pallas_call(
         results_kernel,
         out_shape=[jax.ShapeDtypeStruct(value.shape, value.dtype) for value in values],
-        in_specs=[far] * len(values),
-        out_specs=[far] * len(values),
-        scratch_shapes=[pltpu.SemaphoreType.DMA((len(values),))],
+        in_specs=[vmem] * len(values),
+        out_specs=[vmem] * len(values),
         name="results",
     )(*values)
 

time: 143 us -> 94.8 us (0.66)
  Pallas kernels: 142 us -> 93.9 us
    pallas_call x1, Pallas kernels: 42.8 us -> 2.42 us  [results(): pl.pallas_call(results_kernel, out_shape=[jax.ShapeDtypeStruct(value.shap...]
    pallas_call x1, Pallas kernels: 96.8 us -> 88.7 us  [main(): pl.pallas_call(main_kernel, out_shape=[jax.ShapeDtypeStruct((32, ROWS * B...]
where the time goes in v4:
time: 94.8 us; the launch traced here: 94.5 us
  Pallas kernels  93.9 us (99%)
    pallas_call x1, Pallas kernels, main(): pl.pallas_call(main_kernel, out_shape=[jax.ShapeDtypeStruct((32, ROWS * B...  88.7 us
    pallas_call x1, Pallas kernels, prepare(): pl.pallas_call(prepare_kernel, out_shape=jax.ShapeDtypeStruct((8, WIDE),...  2.76 us
    pallas_call x1, Pallas kernels, results(): pl.pallas_call(results_kernel, out_shape=[jax.ShapeDtypeStruct(value.shap...  2.42 us

profile of v4, /device:TPU:1, one launch (start us, length us, event | category | flops | bytes accessed | tf_op | source)
XLA Modules:
  0.0 94.5 jit_solution(14348188742312909649)
XLA Ops:
  0.6 2.8 %prepare.1.refs_0_ = s32[8,384]{1,0:T(8,128)} custom-call(s32[1,288]{1,0:T(1,128)} %bitcast.9, s32[1,288]{1,0:T(1,128)} %bitcast.10, s32[1,288]{1,0:T(1,128)} %bitcast.11), custom_call_target="tpu_custom_call" | custom-call | tf_op jit(solution)/shard_map/prepare/pallas_call | solution.py:103
  3.4 88.7 %backward.1 = (bf16[32,3072]{1,0:T(8,128)(2,1)}, bf16[18,128,128]{2,1,0:T(8,128)(2,1)}, bf16[18,128,128]{2,1,0:T(8,128)(2,1)}) custom-call(s32[8,384]{1,0:T(8,128)} %prepare.1.refs_0_, bf16[128,3072]{1,0:T(8,128)(2,1)} %refs_1_.1, bf16[128,3072]{1,0:T(8,128)(2,1)} %refs_2_.1, bf16[288,128,128]{2,1,0:T(8,128)(2,1)} %bitcast.7, bf16[288,128,128]{2,1,0:T(8,128)(2,1)} %bitcast.8), custom_call_target="tpu_custom_call" | custom-call | tf_op jit(solution)/shard_map/backward/pallas_call | solution.py:505
  92.1 2.4 %results.1 = (bf16[32,3072]{1,0:T(8,128)(2,1)}, bf16[18,128,128]{2,1,0:T(8,128)(2,1)}, bf16[18,128,128]{2,1,0:T(8,128)(2,1)}) custom-call(bf16[32,3072]{1,0:T(8,128)(2,1)} %get-tuple-element.9.refs_0_, bf16[18,128,128]{2,1,0:T(8,128)(2,1)} %get-tuple-element.10.refs_1_, bf16[18,128,128]{2,1,0:T(8,128)(2,1)} %get-tuple-element.11.refs_2_), custom_call_target="tpu_custom_call" | custom-call | tf_op jit(solution)/shard_map/results/pallas_call | solution.py:530

commit v5 on v4

--- a/solution.py
+++ b/solution.py
@@ -150,9 +150,12 @@
         for load in loads[n]:
             load.wait()
 
-    for group in loads:
-        for load in group:
+    def begin(n):
+        for load in loads[n]:
             load.start()
+
+    for n in (1, 2, 0):
+        begin(n)
     wu[NBLK] = jnp.zeros((B, B), BF)
     wd[NBLK] = jnp.zeros((B, B), BF)
     runs[PAIRS] = jnp.zeros((B, B), BF)
@@ -265,7 +268,9 @@
     for f in range(ROWS):
         xt_own[f] = x_in[f].T
 
-    def products(n, left, weights, axis, count, unroll):
+    def products(n, left, weights, axis, start, stop, total=None):
+        unroll = 12
+
         def body(i, total):
             parts = []
             for j in range(unroll):
@@ -281,7 +286,9 @@
                 runs[i * unroll + j] = total.astype(BF)
             return total
 
-        lax.fori_loop(0, count // unroll, body, jnp.zeros((B, B), F32))
+        if total is None:
+            total = jnp.zeros((B, B), F32)
+        return lax.fori_loop(start, stop, body, total)
 
     def exchange(n, to, mine, into):
         def pick(i, carry):
@@ -303,25 +310,35 @@
         lax.fori_loop(0, 4, own, 0)
 
     loaded(2)
-    products(0, lambda f: x_in[f], wu, 0, PAIRS, 12)
+    begin(3)
+    carried = products(0, lambda f: x_in[f], wu, 0, 0, 7)
     loaded(0)
     pl.semaphore_wait(barrier, len(peers))
     for slots in ((0, 3), (1, 5), (2, 4)):
         for kind in token_kinds:
             for slot in slots:
                 token_send(kind, slot)
+    products(0, lambda f: x_in[f], wu, 0, 7, 14, carried)
     exchange(0, pre_to, pre_ref, pre_in)
-    loaded(3)
-    products(1, lambda f: og_own[f], wd, 1, PAIRS, 12)
-    exchange(1, back_to, back_ref, back_in)
     for kind in token_kinds:
         for slot, source, forward in ((0, 0, 6), (3, 1, 8)):
             token_wait(kind, slot)
             share_send(kind, source)
             token_send(kind, forward)
+    loaded(3)
+    carried = products(1, lambda f: og_own[f], wd, 1, 0, 7)
+    for kind in token_kinds:
         for slot, forward in ((1, 7), (5, 9)):
             token_wait(kind, slot)
             token_send(kind, forward)
+    products(1, lambda f: og_own[f], wd, 1, 7, 14, carried)
+    exchange(1, back_to, back_ref, back_in)
+    for kind in token_kinds:
+        token_wait(kind, 6)
+        token_wait(kind, 8)
+        share_send(kind, 2)
+        share_forward(kind, 0)
+        share_forward(kind, 1)
 
     for c in range(2):
         here = pl.ds(c * CH, CH)
@@ -345,16 +362,9 @@
         ring_out(kind, 1, "r")
         ring_out(kind, 0, "l")
 
-    for kind in token_kinds:
-        token_wait(kind, 6)
-        token_wait(kind, 8)
-        share_send(kind, 2)
-        share_forward(kind, 0)
-        share_forward(kind, 1)
-
     pair_wait("pg", 0)
     pair_wait("pg", 1)
-    products(2, lambda h: pg_own[h], wu, 1, 156, 12)
+    products(2, lambda h: pg_own[h], wu, 1, 0, 13)
     for f in range(ROWS):
         dxp[:, f * B : (f + 1) * B] = runs[tab[5, f]]
     for d in range(1, SIDE):

time: 94.8 us -> 89.9 us (0.948)
  Pallas kernels: 93.9 us -> 89.1 us
    pallas_call x1, Pallas kernels: 88.7 us -> 83.9 us  [main(): pl.pallas_call(main_kernel, out_shape=[jax.ShapeDtypeStruct((32, ROWS * B...]
where the time goes in v5:
time: 89.9 us; the launch traced here: 89.7 us
  Pallas kernels  89.1 us (99%)
    pallas_call x1, Pallas kernels, main(): pl.pallas_call(main_kernel, out_shape=[jax.ShapeDtypeStruct((32, ROWS * B...  83.9 us
    pallas_call x1, Pallas kernels, prepare(): pl.pallas_call(prepare_kernel, out_shape=jax.ShapeDtypeStruct((8, WIDE),...  2.76 us
    pallas_call x1, Pallas kernels, results(): pl.pallas_call(results_kernel, out_shape=[jax.ShapeDtypeStruct(value.shap...  2.42 us

profile of v5, /device:TPU:1, one launch (start us, length us, event | category | flops | bytes accessed | tf_op | source)
XLA Modules:
  0.0 89.7 jit_solution(2092864545205224606)
XLA Ops:
  0.6 2.8 %prepare.1.refs_0_ = s32[8,384]{1,0:T(8,128)} custom-call(s32[1,288]{1,0:T(1,128)} %bitcast.9, s32[1,288]{1,0:T(1,128)} %bitcast.10, s32[1,288]{1,0:T(1,128)} %bitcast.11), custom_call_target="tpu_custom_call" | custom-call | tf_op jit(solution)/shard_map/prepare/pallas_call | solution.py:103
  3.4 83.9 %backward.1 = (bf16[32,3072]{1,0:T(8,128)(2,1)}, bf16[18,128,128]{2,1,0:T(8,128)(2,1)}, bf16[18,128,128]{2,1,0:T(8,128)(2,1)}) custom-call(s32[8,384]{1,0:T(8,128)} %prepare.1.refs_0_, bf16[128,3072]{1,0:T(8,128)(2,1)} %refs_1_.1, bf16[128,3072]{1,0:T(8,128)(2,1)} %refs_2_.1, bf16[288,128,128]{2,1,0:T(8,128)(2,1)} %bitcast.7, bf16[288,128,128]{2,1,0:T(8,128)(2,1)} %bitcast.8), custom_call_target="tpu_custom_call" | custom-call | tf_op jit(solution)/shard_map/backward/pallas_call | solution.py:515
  87.3 2.4 %results.1 = (bf16[32,3072]{1,0:T(8,128)(2,1)}, bf16[18,128,128]{2,1,0:T(8,128)(2,1)}, bf16[18,128,128]{2,1,0:T(8,128)(2,1)}) custom-call(bf16[32,3072]{1,0:T(8,128)(2,1)} %get-tuple-element.9.refs_0_, bf16[18,128,128]{2,1,0:T(8,128)(2,1)} %get-tuple-element.10.refs_1_, bf16[18,128,128]{2,1,0:T(8,128)(2,1)} %get-tuple-element.11.refs_2_), custom_call_target="tpu_custom_call" | custom-call | tf_op jit(solution)/shard_map/results/pallas_call | solution.py:540

commit v6 on v5

--- a/solution.py
+++ b/solution.py
@@ -337,8 +337,6 @@
         token_wait(kind, 6)
         token_wait(kind, 8)
         share_send(kind, 2)
-        share_forward(kind, 0)
-        share_forward(kind, 1)
 
     for c in range(2):
         here = pl.ds(c * CH, CH)
@@ -367,12 +365,9 @@
     products(2, lambda h: pg_own[h], wu, 1, 0, 13)
     for f in range(ROWS):
         dxp[:, f * B : (f + 1) * B] = runs[tab[5, f]]
-    for d in range(1, SIDE):
-        theirs = pl.ds(pl.multiple_of(((col + d) % SIDE) * 32, 32), 32)
-        send(dxp.at[theirs], zin.at[d - 1], z_s.at[d - 1], z_r.at[d - 1], z_peers[d - 1])
-
     for kind in token_kinds:
-        share_forward(kind, 2)
+        share_forward(kind, 0)
+        share_forward(kind, 1)
     for kind in ("pg", "ht"):
         ring_wait(kind, 0)
         ring_forward(kind, "r")
@@ -380,6 +375,11 @@
         ring_wait(kind, 3)
         ring_forward(kind, "l")
         pair_out(kind, 5)
+    for kind in token_kinds:
+        share_forward(kind, 2)
+    for d in range(1, SIDE):
+        theirs = pl.ds(pl.multiple_of(((col + d) % SIDE) * 32, 32), 32)
+        send(dxp.at[theirs], zin.at[d - 1], z_s.at[d - 1], z_r.at[d - 1], z_peers[d - 1])
     for kind in ("pg", "ht"):
         ring_wait(kind, 1)
         pair_out(kind, 3)

time: 89.9 us -> 88.4 us (0.983)
  Pallas kernels: 89.1 us -> 87.5 us
    pallas_call x1, Pallas kernels: 83.9 us -> 82.3 us  [main(): pl.pallas_call(main_kernel, out_shape=[jax.ShapeDtypeStruct((32, ROWS * B...]
where the time goes in v6:
time: 88.4 us; the launch traced here: 88.2 us
  Pallas kernels  87.5 us (99%)
    pallas_call x1, Pallas kernels, main(): pl.pallas_call(main_kernel, out_shape=[jax.ShapeDtypeStruct((32, ROWS * B...  82.3 us
    pallas_call x1, Pallas kernels, prepare(): pl.pallas_call(prepare_kernel, out_shape=jax.ShapeDtypeStruct((8, WIDE),...  2.76 us
    pallas_call x1, Pallas kernels, results(): pl.pallas_call(results_kernel, out_shape=[jax.ShapeDtypeStruct(value.shap...  2.42 us

profile of v6, /device:TPU:1, one launch (start us, length us, event | category | flops | bytes accessed | tf_op | source)
XLA Modules:
  0.0 88.2 jit_solution(17565631019159264252)
XLA Ops:
  0.6 2.8 %prepare.1.refs_0_ = s32[8,384]{1,0:T(8,128)} custom-call(s32[1,288]{1,0:T(1,128)} %bitcast.9, s32[1,288]{1,0:T(1,128)} %bitcast.10, s32[1,288]{1,0:T(1,128)} %bitcast.11), custom_call_target="tpu_custom_call" | custom-call | tf_op jit(solution)/shard_map/prepare/pallas_call | solution.py:103
  3.4 82.3 %backward.1 = (bf16[32,3072]{1,0:T(8,128)(2,1)}, bf16[18,128,128]{2,1,0:T(8,128)(2,1)}, bf16[18,128,128]{2,1,0:T(8,128)(2,1)}) custom-call(s32[8,384]{1,0:T(8,128)} %prepare.1.refs_0_, bf16[128,3072]{1,0:T(8,128)(2,1)} %refs_1_.1, bf16[128,3072]{1,0:T(8,128)(2,1)} %refs_2_.1, bf16[288,128,128]{2,1,0:T(8,128)(2,1)} %bitcast.7, bf16[288,128,128]{2,1,0:T(8,128)(2,1)} %bitcast.8), custom_call_target="tpu_custom_call" | custom-call | tf_op jit(solution)/shard_map/backward/pallas_call | solution.py:515
  85.7 2.4 %results.1 = (bf16[32,3072]{1,0:T(8,128)(2,1)}, bf16[18,128,128]{2,1,0:T(8,128)(2,1)}, bf16[18,128,128]{2,1,0:T(8,128)(2,1)}) custom-call(bf16[32,3072]{1,0:T(8,128)(2,1)} %get-tuple-element.9.refs_0_, bf16[18,128,128]{2,1,0:T(8,128)(2,1)} %get-tuple-element.10.refs_1_, bf16[18,128,128]{2,1,0:T(8,128)(2,1)} %get-tuple-element.11.refs_2_), custom_call_target="tpu_custom_call" | custom-call | tf_op jit(solution)/shard_map/results/pallas_call | solution.py:540

commit v7 on v6

--- a/solution.py
+++ b/solution.py
@@ -26,15 +26,14 @@
 cubic_coef = 0.044715
 
 
-def activate(pre_sum, back_sum):
+def gelu(pre_sum):
     square = pre_sum * pre_sum
-    inner_arg = root_two_pi * (pre_sum + cubic_coef * square * pre_sum)
-    tanh_inner = jnp.tanh(inner_arg)
+    tanh_inner = jnp.tanh(root_two_pi * (pre_sum + cubic_coef * square * pre_sum))
     half = 0.5 * (1.0 + tanh_inner)
     slope = half + 0.5 * pre_sum * (1.0 - tanh_inner * tanh_inner) * root_two_pi * (
         1.0 + 3.0 * cubic_coef * square
     )
-    return pre_sum * half, back_sum * slope
+    return pre_sum * half, slope
 
 
 def dot(left, right, dims):
@@ -331,6 +330,21 @@
         for slot, forward in ((1, 7), (5, 9)):
             token_wait(kind, slot)
             token_send(kind, forward)
+
+    for c in range(2):
+        here = pl.ds(c * CH, CH)
+        arrived(pre_in.at[here], ex_s.at[c], ex_r.at[c], other)
+
+        def hidden_one(i, carry, c=c):
+            pre = pre_ref[c * CH + i].astype(F32) + pre_in[c * CH + i].astype(F32)
+            ht_own[row * ROWS + c * CH + i] = gelu(pre)[0].astype(BF).T
+            return carry
+
+        lax.fori_loop(0, CH, hidden_one, 0)
+        ring_out("ht", c, "rl"[c])
+        pair_out("ht", c)
+    ring_out("ht", 1, "r")
+    ring_out("ht", 0, "l")
     products(1, lambda f: og_own[f], wd, 1, 7, 14, carried)
     exchange(1, back_to, back_ref, back_in)
     for kind in token_kinds:
@@ -340,25 +354,47 @@
 
     for c in range(2):
         here = pl.ds(c * CH, CH)
-        arrived(pre_in.at[here], ex_s.at[c], ex_r.at[c], other)
         arrived(back_in.at[here], ex_s.at[2 + c], ex_r.at[2 + c], other)
 
-        def one(i, carry, c=c):
-            mine = row * ROWS + c * CH + i
+        def grad_one(i, carry, c=c):
             pre = pre_ref[c * CH + i].astype(F32) + pre_in[c * CH + i].astype(F32)
             back = back_ref[c * CH + i].astype(F32) + back_in[c * CH + i].astype(F32)
-            hidden, pre_grad = activate(pre, back)
-            pg_own[mine] = pre_grad.astype(BF)
-            ht_own[mine] = hidden.astype(BF).T
+            pg_own[row * ROWS + c * CH + i] = (back * gelu(pre)[1]).astype(BF)
             return carry
 
-        lax.fori_loop(0, CH, one, 0)
-        for kind in ("pg", "ht"):
-            ring_out(kind, c, "rl"[c])
-            pair_out(kind, c)
-    for kind in ("pg", "ht"):
-        ring_out(kind, 1, "r")
-        ring_out(kind, 0, "l")
+        lax.fori_loop(0, CH, grad_one, 0)
+        ring_out("pg", c, "rl"[c])
+        pair_out("pg", c)
+    ring_out("pg", 1, "r")
+    ring_out("pg", 0, "l")
+
+    def pass_on(kind):
+        ring_wait(kind, 0)
+        ring_forward(kind, "r")
+        pair_out(kind, 2)
+        ring_wait(kind, 3)
+        ring_forward(kind, "l")
+        pair_out(kind, 5)
+
+    def pass_rest(kind):
+        ring_wait(kind, 1)
+        pair_out(kind, 3)
+        ring_wait(kind, 2)
+        pair_out(kind, 4)
+
+    def pass_far(kind):
+        for slot in (4, 6, 5, 7):
+            ring_wait(kind, slot)
+            pair_out(kind, slot + 2)
+
+    def tokens_in_place(kind):
+        for slot in (2, 4, 7, 9):
+            token_wait(kind, slot)
+        for source in range(3):
+            share_wait(kind, source, 1 - kind[0])
+            share_wait(kind, source, 2)
+
+    pass_on("ht")
 
     pair_wait("pg", 0)
     pair_wait("pg", 1)
@@ -368,39 +404,18 @@
     for kind in token_kinds:
         share_forward(kind, 0)
         share_forward(kind, 1)
-    for kind in ("pg", "ht"):
-        ring_wait(kind, 0)
-        ring_forward(kind, "r")
-        pair_out(kind, 2)
-        ring_wait(kind, 3)
-        ring_forward(kind, "l")
-        pair_out(kind, 5)
+    pass_rest("ht")
+    pass_on("pg")
     for kind in token_kinds:
         share_forward(kind, 2)
     for d in range(1, SIDE):
         theirs = pl.ds(pl.multiple_of(((col + d) % SIDE) * 32, 32), 32)
         send(dxp.at[theirs], zin.at[d - 1], z_s.at[d - 1], z_r.at[d - 1], z_peers[d - 1])
-    for kind in ("pg", "ht"):
-        ring_wait(kind, 1)
-        pair_out(kind, 3)
-        ring_wait(kind, 2)
-        pair_out(kind, 4)
-    for kind in token_kinds:
-        for slot in (2, 4, 7, 9):
-            token_wait(kind, slot)
-        for source in range(3):
-            share_wait(kind, source, 1 - kind[0])
-            share_wait(kind, source, 2)
-    for slot in (4, 6, 5, 7):
-        for kind in ("pg", "ht"):
-            ring_wait(kind, slot)
-            pair_out(kind, slot + 2)
-    for kind in ("ht",):
-        for slot in range(2):
-            pair_wait(kind, slot)
-    for slot in range(2, 10):
-        for kind in ("pg", "ht"):
-            pair_wait(kind, slot)
+    pass_far("ht")
+    pass_rest("pg")
+    for slot in range(10):
+        pair_wait("ht", slot)
+    tokens_in_place(token_kinds[1])
 
     def up_block(s):
         e = tab[6, s]
@@ -441,26 +456,46 @@
         (0, up_block, up_base, y_right, y_left, uf_s, ur_s, ul_s, ua_t, ub_t, ul_v, ur_v, u_acc, up_out),
         (1, dn_block, dn_base, x_right, x_left, df_s, dr_s, dl_s, da_t, db_t, dl_v, dr_v, d_acc, dn_out),
     )
-    for n, block, base, to_right, to_left, f_s, r_s, l_s, a_t, b_t, l_v, r_v, acc, out in sides:
-        fill(block, base(2), f_s, 0)
-        send(f_s.at[early], a_t, rs_s.at[n, 0], rs_r.at[n, 0], to_right)
-        fill(block, base(2), f_s, half)
-        send(f_s.at[late], b_t, rs_s.at[n, 1], rs_r.at[n, 1], to_left)
-    for n, block, base, to_right, to_left, f_s, r_s, l_s, a_t, b_t, l_v, r_v, acc, out in sides:
-        fill(block, base(1), r_s, half)
-        send(r_s.at[late], l_v.at[late], rs_s.at[n, 2], rs_r.at[n, 2], to_right)
-        fill(block, base(3), l_s, 0)
-        send(l_s.at[early], r_v.at[early], rs_s.at[n, 3], rs_r.at[n, 3], to_left)
-    for n, block, base, to_right, to_left, f_s, r_s, l_s, a_t, b_t, l_v, r_v, acc, out in sides:
+    def make(side, piece):
+        _, block, base, _, _, f_s, r_s, l_s, _, _, _, _, acc, _ = side
+        d, into, first = ((2, f_s, 0), (2, f_s, half), (1, r_s, half), (3, l_s, 0), (0, acc, 0), (0, acc, half))[piece]
+        fill(block, base(d), into, first)
+
+    def ship(side, piece):
+        n, _, _, to_right, to_left, f_s, r_s, l_s, a_t, b_t, l_v, r_v, _, _ = side
+        src, dst, peer = (
+            (f_s.at[early], a_t, to_right),
+            (f_s.at[late], b_t, to_left),
+            (r_s.at[late], l_v.at[late], to_right),
+            (l_s.at[early], r_v.at[early], to_left),
+        )[piece]
+        send(src, dst, rs_s.at[n, piece], rs_r.at[n, piece], peer)
+
+    def finish(side):
+        n, block, base, to_right, to_left, _, r_s, l_s, a_t, b_t, l_v, r_v, _, _ = side
         arrived(a_t, rs_s.at[n, 0], rs_r.at[n, 0], to_left)
         fill(block, base(1), r_s, 0, a_t)
         send(r_s.at[early], l_v.at[early], rs_s.at[n, 4], rs_r.at[n, 4], to_right)
         arrived(b_t, rs_s.at[n, 1], rs_r.at[n, 1], to_right)
         fill(block, base(3), l_s, half, b_t)
         send(l_s.at[late], r_v.at[late], rs_s.at[n, 5], rs_r.at[n, 5], to_left)
-    for n, block, base, to_right, to_left, f_s, r_s, l_s, a_t, b_t, l_v, r_v, acc, out in sides:
-        fill(block, base(0), acc, 0)
-        fill(block, base(0), acc, half)
+
+    up_side, dn_side = sides
+    for piece in range(6):
+        make(dn_side, piece)
+    pass_far("pg")
+    for piece in range(4):
+        ship(dn_side, piece)
+    tokens_in_place(token_kinds[0])
+    for slot in range(2, 10):
+        pair_wait("pg", slot)
+    for piece in range(4):
+        make(up_side, piece)
+        ship(up_side, piece)
+    finish(dn_side)
+    finish(up_side)
+    make(up_side, 4)
+    make(up_side, 5)
 
     for d in range(1, SIDE):
         arrived(zin.at[d - 1], z_s.at[d - 1], z_r.at[d - 1], z_peers[d - 1])

time: 88.4 us -> 87.2 us (0.986)
  Pallas kernels: 87.5 us -> 86.3 us
    pallas_call x1, Pallas kernels: 82.3 us -> 81.1 us  [main(): pl.pallas_call(main_kernel, out_shape=[jax.ShapeDtypeStruct((32, ROWS * B...]
where the time goes in v7:
time: 87.2 us; the launch traced here: 86.9 us
  Pallas kernels  86.3 us (99%)
    pallas_call x1, Pallas kernels, main(): pl.pallas_call(main_kernel, out_shape=[jax.ShapeDtypeStruct((32, ROWS * B...  81.1 us
    pallas_call x1, Pallas kernels, prepare(): pl.pallas_call(prepare_kernel, out_shape=jax.ShapeDtypeStruct((8, WIDE),...  2.76 us
    pallas_call x1, Pallas kernels, results(): pl.pallas_call(results_kernel, out_shape=[jax.ShapeDtypeStruct(value.shap...  2.42 us

profile of v7, /device:TPU:1, one launch (start us, length us, event | category | flops | bytes accessed | tf_op | source)
XLA Modules:
  0.0 86.9 jit_solution(14694766648711438256)
XLA Ops:
  0.6 2.8 %prepare.1.refs_0_ = s32[8,384]{1,0:T(8,128)} custom-call(s32[1,288]{1,0:T(1,128)} %bitcast.9, s32[1,288]{1,0:T(1,128)} %bitcast.10, s32[1,288]{1,0:T(1,128)} %bitcast.11), custom_call_target="tpu_custom_call" | custom-call | tf_op jit(solution)/shard_map/prepare/pallas_call | solution.py:102
  3.4 81.1 %backward.1 = (bf16[32,3072]{1,0:T(8,128)(2,1)}, bf16[18,128,128]{2,1,0:T(8,128)(2,1)}, bf16[18,128,128]{2,1,0:T(8,128)(2,1)}) custom-call(s32[8,384]{1,0:T(8,128)} %prepare.1.refs_0_, bf16[128,3072]{1,0:T(8,128)(2,1)} %refs_1_.1, bf16[128,3072]{1,0:T(8,128)(2,1)} %refs_2_.1, bf16[288,128,128]{2,1,0:T(8,128)(2,1)} %bitcast.7, bf16[288,128,128]{2,1,0:T(8,128)(2,1)} %bitcast.8), custom_call_target="tpu_custom_call" | custom-call | tf_op jit(solution)/shard_map/backward/pallas_call | solution.py:550
  84.5 2.4 %results.1 = (bf16[32,3072]{1,0:T(8,128)(2,1)}, bf16[18,128,128]{2,1,0:T(8,128)(2,1)}, bf16[18,128,128]{2,1,0:T(8,128)(2,1)}) custom-call(bf16[32,3072]{1,0:T(8,128)(2,1)} %get-tuple-element.9.refs_0_, bf16[18,128,128]{2,1,0:T(8,128)(2,1)} %get-tuple-element.10.refs_1_, bf16[18,128,128]{2,1,0:T(8,128)(2,1)} %get-tuple-element.11.refs_2_), custom_call_target="tpu_custom_call" | custom-call | tf_op jit(solution)/shard_map/results/pallas_call | solution.py:575

commit v8 on v7

--- a/solution.py
+++ b/solution.py
@@ -40,75 +40,71 @@
     return lax.dot_general(left, right, dims, preferred_element_type=F32)
 
 
-def prepare_kernel(up_ref, dn_ref, own_ref, out_ref):
+def make_tables(up_ref, dn_ref, own_ref, out_ref):
     def iota(shape, axis):
         return lax.broadcasted_iota(jnp.int32, shape, axis)
 
     square = (NBLK, NBLK)
     sub, lane = iota(square, 0), iota(square, 1)
     wide = iota((NBLK, WIDE), 1)
-    one, zero = jnp.float32(1), jnp.float32(0)
+
+    def total(values, axis):
+        return jnp.sum(values, axis=axis, keepdims=True)
 
     def count(mask, axis):
-        return jnp.sum(jnp.where(mask, one, zero), axis=axis, keepdims=True)
+        return total(jnp.where(mask, 1, 0), axis)
 
     def column(row):
-        picked = jnp.where(sub == lane, jnp.broadcast_to(row, square).astype(F32), zero)
-        return jnp.sum(picked, axis=1, keepdims=True).astype(jnp.int32)
-
-    def pairs(e_row, e_col, split, segment, operand):
+        return total(jnp.where(sub == lane, jnp.broadcast_to(row, square), 0), 1)
+
+    def pairs(e_row, e_col, segment, operand):
         seg_row, seg_col = segment(e_row), segment(e_col)
         same = seg_col == seg_row
-        turn = count(same & (lane < sub), 1).astype(jnp.int32)
+        turn = count(same & (lane < sub), 1)
         even = (turn & 1) == 0
-        turn_row = count(same & (sub < lane), 0).astype(jnp.int32)
-        even_row = (turn_row & 1) == 0
-        offset = count((seg_row < seg_col) & even_row, 1).astype(jnp.int32)
+        even_row = (count(same & (sub < lane), 0) & 1) == 0
+        offset = count((seg_row < seg_col) & even_row, 1)
         place = 2 * (offset + (turn >> 1)) + (turn & 1)
         block = NBLK - iota((NBLK, 1), 0)
         value = block * 64 + operand(e_col) + jnp.where(turn >= 2, 65536, 0)
-        table = jnp.sum(jnp.where(place == wide, value.astype(F32), zero), axis=0, keepdims=True)
+        table = total(jnp.where(place == wide, value, 0), 0)
         through = count((seg_col <= wide) & even, 0)
         here = count((seg_col == wide) & even, 0)
-        last = jnp.where(here > zero, through - one, jnp.float32(PAIRS))
-        return table.astype(jnp.int32), last.astype(jnp.int32)
+        return table, jnp.where(here > 0, through - 1, PAIRS)
 
     up_row, dn_row, owner_row = up_ref[...], dn_ref[...], own_ref[...]
     up_col, dn_col, owner_col = column(up_row), column(dn_row), column(owner_row)
 
     def owned(value):
-        picked = jnp.where(owner_col == wide, value.astype(F32), zero)
-        return jnp.sum(picked, axis=0, keepdims=True).astype(jnp.int32)
-
-    def div(value, by):
-        return (value.astype(F32) * jnp.float32(1.0 / by) + jnp.float32(0.5 / by)).astype(jnp.int32)
-
-    def rem(value, by):
-        return value - div(value, by) * by
-
-    t0, l0 = pairs(up_row, up_col, COLS, lambda e: rem(e, COLS), lambda e: div(e, COLS))
-    t1, l1 = pairs(dn_row, dn_col, ROWS, lambda e: div(e, ROWS), lambda e: rem(e, ROWS))
-    t2, l2 = pairs(up_row, up_col, COLS, lambda e: div(e, COLS), lambda e: rem(e, COLS))
+        return total(jnp.where(owner_col == wide, value, 0), 0)
+
+    def by_cols(value):
+        return (value * 1366) >> 16
+
+    def by_rows(value):
+        return (value * 2731) >> 16
+
+    def in_cols(value):
+        return value - by_cols(value) * COLS
+
+    def in_rows(value):
+        return value - by_rows(value) * ROWS
+
+    t0, l0 = pairs(up_row, up_col, in_cols, by_cols)
+    t1, l1 = pairs(dn_row, dn_col, by_rows, in_rows)
+    t2, l2 = pairs(up_row, up_col, by_cols, in_cols)
     rows = (
         t0, t1, t2, l0, l1, l2,
-        owned(div(up_col, COLS) * 64 + rem(up_col, COLS)),
-        owned(rem(dn_col, ROWS) * 64 + div(dn_col, ROWS)),
+        owned(by_cols(up_col) * 64 + in_cols(up_col)),
+        owned(in_rows(dn_col) * 64 + by_rows(dn_col)),
     )
     for n, value in enumerate(rows):
         out_ref[n : n + 1, :] = value
 
 
-def prepare(up, down, owner):
-    return pl.pallas_call(
-        prepare_kernel,
-        out_shape=jax.ShapeDtypeStruct((8, WIDE), jnp.int32),
-        name="prepare",
-    )(up, down, owner)
-
-
 def main_kernel(*refs):
-    tab, x_hbm, g_hbm, wu_hbm, wd_hbm = refs[:5]
-    dx_out, up_out, dn_out = refs[5:8]
+    up_ref, dn_ref, own_ref, x_hbm, g_hbm, wu_hbm, wd_hbm = refs[:7]
+    dx_out, up_out, dn_out = refs[7:10]
     (
         x_in, og_own, xt_own, wu, wd, runs,
         pre_ref, back_ref, pre_to, back_to, pre_in, back_in, pg_own, ht_own,
@@ -118,7 +114,8 @@
         uf_s, ur_s, ul_s, ua_t, ub_t, ul_v, ur_v, u_acc,
         df_s, dr_s, dl_s, da_t, db_t, dl_v, dr_v, d_acc,
         ex_s, ex_r, ag_s, ag_r, pa_s, pa_r, rs_s, rs_r, z_s, z_r, in_s, col_s, to_s, to_r, sh_s, sh_r,
-    ) = refs[8:]
+        made, tab, tab_s,
+    ) = refs[10:]
     dp, row, col = lax.axis_index("dp"), lax.axis_index("row"), lax.axis_index("col")
     y, x = dp // SIDE, dp % SIDE
     other = (dp, 1 - row, col)
@@ -155,6 +152,9 @@
 
     for n in (1, 2, 0):
         begin(n)
+    make_tables(up_ref, dn_ref, own_ref, made)
+    tables = pltpu.make_async_copy(made, tab, tab_s)
+    tables.start()
     wu[NBLK] = jnp.zeros((B, B), BF)
     wd[NBLK] = jnp.zeros((B, B), BF)
     runs[PAIRS] = jnp.zeros((B, B), BF)
@@ -268,7 +268,7 @@
         xt_own[f] = x_in[f].T
 
     def products(n, left, weights, axis, start, stop, total=None):
-        unroll = 12
+        unroll = 28
 
         def body(i, total):
             parts = []
@@ -308,16 +308,17 @@
             send(to.at[here], into.at[here], ex_s.at[2 * n + c], ex_r.at[2 * n + c], other)
         lax.fori_loop(0, 4, own, 0)
 
+    tables.wait()
     loaded(2)
     begin(3)
-    carried = products(0, lambda f: x_in[f], wu, 0, 0, 7)
+    carried = products(0, lambda f: x_in[f], wu, 0, 0, 3)
     loaded(0)
     pl.semaphore_wait(barrier, len(peers))
     for slots in ((0, 3), (1, 5), (2, 4)):
         for kind in token_kinds:
             for slot in slots:
                 token_send(kind, slot)
-    products(0, lambda f: x_in[f], wu, 0, 7, 14, carried)
+    products(0, lambda f: x_in[f], wu, 0, 3, 6, carried)
     exchange(0, pre_to, pre_ref, pre_in)
     for kind in token_kinds:
         for slot, source, forward in ((0, 0, 6), (3, 1, 8)):
@@ -325,7 +326,7 @@
             share_send(kind, source)
             token_send(kind, forward)
     loaded(3)
-    carried = products(1, lambda f: og_own[f], wd, 1, 0, 7)
+    carried = products(1, lambda f: og_own[f], wd, 1, 0, 3)
     for kind in token_kinds:
         for slot, forward in ((1, 7), (5, 9)):
             token_wait(kind, slot)
@@ -345,7 +346,7 @@
         pair_out("ht", c)
     ring_out("ht", 1, "r")
     ring_out("ht", 0, "l")
-    products(1, lambda f: og_own[f], wd, 1, 7, 14, carried)
+    products(1, lambda f: og_own[f], wd, 1, 3, 6, carried)
     exchange(1, back_to, back_ref, back_in)
     for kind in token_kinds:
         token_wait(kind, 6)
@@ -398,7 +399,7 @@
 
     pair_wait("pg", 0)
     pair_wait("pg", 1)
-    products(2, lambda h: pg_own[h], wu, 1, 0, 13)
+    products(2, lambda h: pg_own[h], wu, 1, 0, 6)
     for f in range(ROWS):
         dxp[:, f * B : (f + 1) * B] = runs[tab[5, f]]
     for kind in token_kinds:
@@ -518,7 +519,7 @@
         copy.wait_send()
 
 
-def main(table, x, g, wu, wd):
+def main(up, dn, owner, x, g, wu, wd):
     vmem = pl.BlockSpec(memory_space=pltpu.VMEM)
     far = pl.BlockSpec(memory_space=pl.ANY)
 
@@ -546,6 +547,7 @@
         + [dma((2,)), dma((2, ROWS))]
         + [dma((2, 10))] * 2
         + [dma((2, 3, 3))] * 2
+        + [pltpu.VMEM((8, WIDE), jnp.int32), pltpu.SMEM((8, WIDE), jnp.int32), dma(())]
     )
     return pl.pallas_call(
         main_kernel,
@@ -554,14 +556,14 @@
             jax.ShapeDtypeStruct((SHARE, B, B), BF),
             jax.ShapeDtypeStruct((SHARE, B, B), BF),
         ],
-        in_specs=[pl.BlockSpec(memory_space=pltpu.SMEM)] + [far] * 4,
+        in_specs=[vmem] * 3 + [far] * 4,
         out_specs=[vmem] * 3,
         scratch_shapes=scratch,
         compiler_params=pltpu.CompilerParams(
             collective_id=0, has_side_effects=True, vmem_limit_bytes=62 * 2**20
         ),
         name="backward",
-    )(table, x, g, wu, wd)
+    )(up, dn, owner, x, g, wu, wd)
 
 
 def results_kernel(*refs):
@@ -582,9 +584,10 @@
 
 
 def shards(tokens_in, out_grad, up_weight, down_weight, up_blocks, down_blocks, owners):
-    table = prepare(up_blocks[0], down_blocks[0], owners[0])
     input_grad, up_grad, down_grad = results(
-        *main(table, tokens_in, out_grad, up_weight[0, 0], down_weight[0, 0])
+        *main(
+            up_blocks[0], down_blocks[0], owners[0], tokens_in, out_grad, up_weight[0, 0], down_weight[0, 0]
+        )
     )
     return input_grad, up_grad[None, None], down_grad[None, None]
 

time: 87.2 us -> 83.1 us (0.953)
  Pallas kernels: 86.3 us -> 81.7 us
    pallas_call x1 -> x0, Pallas kernels: 2.76 us -> none  [prepare(): pl.pallas_call(prepare_kernel, out_shape=jax.ShapeDtypeStruct((8, WIDE),...]
    pallas_call x1, Pallas kernels: 81.1 us -> 79.3 us  [main(): pl.pallas_call(main_kernel, out_shape=[jax.ShapeDtypeStruct((32, ROWS * B...]
where the time goes in v8:
time: 83.1 us; the launch traced here: 82.3 us
  Pallas kernels  81.7 us (98%)
    pallas_call x1, Pallas kernels, main(): pl.pallas_call(main_kernel, out_shape=[jax.ShapeDtypeStruct((32, ROWS * B...  79.3 us
    pallas_call x1, Pallas kernels, results(): pl.pallas_call(results_kernel, out_shape=[jax.ShapeDtypeStruct(value.shap...  2.42 us

profile of v8, /device:TPU:1, one launch (start us, length us, event | category | flops | bytes accessed | tf_op | source)
XLA Modules:
  0.0 82.3 jit_solution(15158889203904829095)
XLA Ops:
  0.6 79.3 %backward.1 = (bf16[32,3072]{1,0:T(8,128)(2,1)}, bf16[18,128,128]{2,1,0:T(8,128)(2,1)}, bf16[18,128,128]{2,1,0:T(8,128)(2,1)}) custom-call(s32[1,288]{1,0:T(1,128)} %bitcast.9, s32[1,288]{1,0:T(1,128)} %bitcast.10, s32[1,288]{1,0:T(1,128)} %bitcast.11, bf16[128,3072]{1,0:T(8,128)(2,1)} %refs_3_.1, bf16[128,3072]{1,0:T(8,128)(2,1)} %refs_4_.1, ...), custom_call_target="tpu_custom_call" | custom-call | tf_op jit(solution)/shard_map/backward/pallas_call | solution.py:552
  79.9 2.4 %results.1 = (bf16[32,3072]{1,0:T(8,128)(2,1)}, bf16[18,128,128]{2,1,0:T(8,128)(2,1)}, bf16[18,128,128]{2,1,0:T(8,128)(2,1)}) custom-call(bf16[32,3072]{1,0:T(8,128)(2,1)} %get-tuple-element.9.refs_0_, bf16[18,128,128]{2,1,0:T(8,128)(2,1)} %get-tuple-element.10.refs_1_, bf16[18,128,128]{2,1,0:T(8,128)(2,1)} %get-tuple-element.11.refs_2_), custom_call_target="tpu_custom_call" | custom-call | tf_op jit(solution)/shard_map/results/pallas_call | solution.py:577

commit v9 on v8

--- a/solution.py
+++ b/solution.py
@@ -311,26 +311,21 @@
     tables.wait()
     loaded(2)
     begin(3)
-    carried = products(0, lambda f: x_in[f], wu, 0, 0, 3)
+    products(0, lambda f: x_in[f], wu, 0, 0, 6)
     loaded(0)
     pl.semaphore_wait(barrier, len(peers))
+    exchange(0, pre_to, pre_ref, pre_in)
     for slots in ((0, 3), (1, 5), (2, 4)):
         for kind in token_kinds:
             for slot in slots:
                 token_send(kind, slot)
-    products(0, lambda f: x_in[f], wu, 0, 3, 6, carried)
-    exchange(0, pre_to, pre_ref, pre_in)
+    loaded(3)
+    carried = products(1, lambda f: og_own[f], wd, 1, 0, 3)
     for kind in token_kinds:
         for slot, source, forward in ((0, 0, 6), (3, 1, 8)):
             token_wait(kind, slot)
             share_send(kind, source)
             token_send(kind, forward)
-    loaded(3)
-    carried = products(1, lambda f: og_own[f], wd, 1, 0, 3)
-    for kind in token_kinds:
-        for slot, forward in ((1, 7), (5, 9)):
-            token_wait(kind, slot)
-            token_send(kind, forward)
 
     for c in range(2):
         here = pl.ds(c * CH, CH)
@@ -346,12 +341,12 @@
         pair_out("ht", c)
     ring_out("ht", 1, "r")
     ring_out("ht", 0, "l")
+    for kind in token_kinds:
+        for slot, forward in ((1, 7), (5, 9)):
+            token_wait(kind, slot)
+            token_send(kind, forward)
     products(1, lambda f: og_own[f], wd, 1, 3, 6, carried)
     exchange(1, back_to, back_ref, back_in)
-    for kind in token_kinds:
-        token_wait(kind, 6)
-        token_wait(kind, 8)
-        share_send(kind, 2)
 
     for c in range(2):
         here = pl.ds(c * CH, CH)
@@ -395,6 +390,10 @@
             share_wait(kind, source, 1 - kind[0])
             share_wait(kind, source, 2)
 
+    for kind in token_kinds:
+        token_wait(kind, 6)
+        token_wait(kind, 8)
+        share_send(kind, 2)
     pass_on("ht")
 
     pair_wait("pg", 0)
@@ -507,14 +506,27 @@
     for n, block, base, to_right, to_left, f_s, r_s, l_s, a_t, b_t, l_v, r_v, acc, out in sides:
         arrived(l_v.at[late], rs_s.at[n, 2], rs_r.at[n, 2], to_left)
         arrived(r_v.at[early], rs_s.at[n, 3], rs_r.at[n, 3], to_right)
+
+        def partial(i, carry, acc=acc, l_v=l_v, r_v=r_v):
+            for j in range(3):
+                at = 3 * i + j
+                acc[at] = acc[at] + r_v[at].astype(F32)
+                acc[half + at] = acc[half + at] + l_v[half + at].astype(F32)
+            return carry
+
+        lax.fori_loop(0, half // 3, partial, 0)
+    for n, block, base, to_right, to_left, f_s, r_s, l_s, a_t, b_t, l_v, r_v, acc, out in sides:
         arrived(l_v.at[early], rs_s.at[n, 4], rs_r.at[n, 4], to_left)
         arrived(r_v.at[late], rs_s.at[n, 5], rs_r.at[n, 5], to_right)
 
-        def total(i, carry, acc=acc, l_v=l_v, r_v=r_v, out=out):
-            out[i] = (acc[i] + l_v[i].astype(F32) + r_v[i].astype(F32)).astype(BF)
+        def final(i, carry, acc=acc, l_v=l_v, r_v=r_v, out=out):
+            for j in range(3):
+                at = 3 * i + j
+                out[at] = (acc[at] + l_v[at].astype(F32)).astype(BF)
+                out[half + at] = (acc[half + at] + r_v[half + at].astype(F32)).astype(BF)
             return carry
 
-        lax.fori_loop(0, SHARE, total, 0)
+        lax.fori_loop(0, half // 3, final, 0)
     for copy in started:
         copy.wait_send()
 
@@ -567,18 +579,28 @@
 
 
 def results_kernel(*refs):
-    count = len(refs) // 2
+    count = (len(refs) - 2) // 3
+    in_sem, out_sem = refs[-2:]
+    ins = [pltpu.make_async_copy(refs[n], refs[2 * count + n], in_sem.at[n]) for n in range(count)]
+    outs = [pltpu.make_async_copy(refs[2 * count + n], refs[count + n], out_sem.at[n]) for n in range(count)]
+    for copy in ins:
+        copy.start()
     for n in range(count):
-        refs[count + n][...] = refs[n][...]
+        ins[n].wait()
+        outs[n].start()
+    for copy in outs:
+        copy.wait()
 
 
 def results(*values):
-    vmem = pl.BlockSpec(memory_space=pltpu.VMEM)
+    far = pl.BlockSpec(memory_space=pl.ANY)
     return pl.pallas_call(
         results_kernel,
         out_shape=[jax.ShapeDtypeStruct(value.shape, value.dtype) for value in values],
-        in_specs=[vmem] * len(values),
-        out_specs=[vmem] * len(values),
+        in_specs=[far] * len(values),
+        out_specs=[far] * len(values),
+        scratch_shapes=[pltpu.VMEM(value.shape, value.dtype) for value in values]
+        + [pltpu.SemaphoreType.DMA((len(values),))] * 2,
         name="results",
     )(*values)
 

time: 83.1 us -> 84.3 us (1.014)
  Pallas kernels: 81.7 us -> 83.5 us
    pallas_call x1, Pallas kernels: 79.3 us -> 81.2 us  [main(): pl.pallas_call(main_kernel, out_shape=[jax.ShapeDtypeStruct((32, ROWS * B...]
where the time goes in v9:
time: 84.3 us; the launch traced here: 84.1 us
  Pallas kernels  83.5 us (99%)
    pallas_call x1, Pallas kernels, main(): pl.pallas_call(main_kernel, out_shape=[jax.ShapeDtypeStruct((32, ROWS * B...  81.2 us
    pallas_call x1, Pallas kernels, results(): pl.pallas_call(results_kernel, out_shape=[jax.ShapeDtypeStruct(value.shap...  2.23 us

profile of v9, /device:TPU:1, one launch (start us, length us, event | category | flops | bytes accessed | tf_op | source)
XLA Modules:
  0.0 84.1 jit_solution(6895243214540745048)
XLA Ops:
  0.6 81.2 %backward.1 = (bf16[32,3072]{1,0:T(8,128)(2,1)}, bf16[18,128,128]{2,1,0:T(8,128)(2,1)}, bf16[18,128,128]{2,1,0:T(8,128)(2,1)}) custom-call(s32[1,288]{1,0:T(1,128)} %bitcast.9, s32[1,288]{1,0:T(1,128)} %bitcast.10, s32[1,288]{1,0:T(1,128)} %bitcast.11, bf16[128,3072]{1,0:T(8,128)(2,1)} %refs_3_.1, bf16[128,3072]{1,0:T(8,128)(2,1)} %refs_4_.1, ...), custom_call_target="tpu_custom_call" | custom-call | tf_op jit(solution)/shard_map/backward/pallas_call | solution.py:564
  81.9 2.2 %results.1 = (bf16[32,3072]{1,0:T(8,128)(2,1)}, bf16[18,128,128]{2,1,0:T(8,128)(2,1)}, bf16[18,128,128]{2,1,0:T(8,128)(2,1)}) custom-call(bf16[32,3072]{1,0:T(8,128)(2,1)} %get-tuple-element.9.refs_0_, bf16[18,128,128]{2,1,0:T(8,128)(2,1)} %get-tuple-element.10.refs_1_, bf16[18,128,128]{2,1,0:T(8,128)(2,1)} %get-tuple-element.11.refs_2_), custom_call_target="tpu_custom_call" | custom-call | tf_op jit(solution)/shard_map/results/pallas_call | solution.py:597

commit v10 on v9

--- a/solution.py
+++ b/solution.py
@@ -311,21 +311,26 @@
     tables.wait()
     loaded(2)
     begin(3)
-    products(0, lambda f: x_in[f], wu, 0, 0, 6)
     loaded(0)
     pl.semaphore_wait(barrier, len(peers))
-    exchange(0, pre_to, pre_ref, pre_in)
     for slots in ((0, 3), (1, 5), (2, 4)):
         for kind in token_kinds:
             for slot in slots:
                 token_send(kind, slot)
-    loaded(3)
-    carried = products(1, lambda f: og_own[f], wd, 1, 0, 3)
+    carried = products(0, lambda f: x_in[f], wu, 0, 0, 3)
+    products(0, lambda f: x_in[f], wu, 0, 3, 6, carried)
+    exchange(0, pre_to, pre_ref, pre_in)
     for kind in token_kinds:
         for slot, source, forward in ((0, 0, 6), (3, 1, 8)):
             token_wait(kind, slot)
             share_send(kind, source)
             token_send(kind, forward)
+    loaded(3)
+    carried = products(1, lambda f: og_own[f], wd, 1, 0, 3)
+    for kind in token_kinds:
+        for slot, forward in ((1, 7), (5, 9)):
+            token_wait(kind, slot)
+            token_send(kind, forward)
 
     for c in range(2):
         here = pl.ds(c * CH, CH)
@@ -341,12 +346,12 @@
         pair_out("ht", c)
     ring_out("ht", 1, "r")
     ring_out("ht", 0, "l")
-    for kind in token_kinds:
-        for slot, forward in ((1, 7), (5, 9)):
-            token_wait(kind, slot)
-            token_send(kind, forward)
     products(1, lambda f: og_own[f], wd, 1, 3, 6, carried)
     exchange(1, back_to, back_ref, back_in)
+    for kind in token_kinds:
+        token_wait(kind, 6)
+        token_wait(kind, 8)
+        share_send(kind, 2)
 
     for c in range(2):
         here = pl.ds(c * CH, CH)
@@ -390,10 +395,6 @@
             share_wait(kind, source, 1 - kind[0])
             share_wait(kind, source, 2)
 
-    for kind in token_kinds:
-        token_wait(kind, 6)
-        token_wait(kind, 8)
-        share_send(kind, 2)
     pass_on("ht")
 
     pair_wait("pg", 0)

time: 84.3 us -> 80.6 us (0.956)
  Pallas kernels: 83.5 us -> 79.4 us
    pallas_call x1, Pallas kernels: 81.2 us -> 77.2 us  [main(): pl.pallas_call(main_kernel, out_shape=[jax.ShapeDtypeStruct((32, ROWS * B...]
where the time goes in v10:
time: 80.6 us; the launch traced here: 80 us
  Pallas kernels  79.4 us (99%)
    pallas_call x1, Pallas kernels, main(): pl.pallas_call(main_kernel, out_shape=[jax.ShapeDtypeStruct((32, ROWS * B...  77.2 us
    pallas_call x1, Pallas kernels, results(): pl.pallas_call(results_kernel, out_shape=[jax.ShapeDtypeStruct(value.shap...  2.23 us

profile of v10, /device:TPU:1, one launch (start us, length us, event | category | flops | bytes accessed | tf_op | source)
XLA Modules:
  0.0 80.0 jit_solution(15278404948866455405)
XLA Ops:
  0.6 77.2 %backward.1 = (bf16[32,3072]{1,0:T(8,128)(2,1)}, bf16[18,128,128]{2,1,0:T(8,128)(2,1)}, bf16[18,128,128]{2,1,0:T(8,128)(2,1)}) custom-call(s32[1,288]{1,0:T(1,128)} %bitcast.9, s32[1,288]{1,0:T(1,128)} %bitcast.10, s32[1,288]{1,0:T(1,128)} %bitcast.11, bf16[128,3072]{1,0:T(8,128)(2,1)} %refs_3_.1, bf16[128,3072]{1,0:T(8,128)(2,1)} %refs_4_.1, ...), custom_call_target="tpu_custom_call" | custom-call | tf_op jit(solution)/shard_map/backward/pallas_call | solution.py:565
  77.8 2.2 %results.1 = (bf16[32,3072]{1,0:T(8,128)(2,1)}, bf16[18,128,128]{2,1,0:T(8,128)(2,1)}, bf16[18,128,128]{2,1,0:T(8,128)(2,1)}) custom-call(bf16[32,3072]{1,0:T(8,128)(2,1)} %get-tuple-element.9.refs_0_, bf16[18,128,128]{2,1,0:T(8,128)(2,1)} %get-tuple-element.10.refs_1_, bf16[18,128,128]{2,1,0:T(8,128)(2,1)} %get-tuple-element.11.refs_2_), custom_call_target="tpu_custom_call" | custom-call | tf_op jit(solution)/shard_map/results/pallas_call | solution.py:598

commit v11 on v10

--- a/solution.py
+++ b/solution.py
@@ -266,6 +266,12 @@
     loaded(1)
     for f in range(ROWS):
         xt_own[f] = x_in[f].T
+    loaded(0)
+    pl.semaphore_wait(barrier, len(peers))
+    for slots in ((0, 3), (1, 5), (2, 4)):
+        for kind in token_kinds:
+            for slot in slots:
+                token_send(kind, slot)
 
     def products(n, left, weights, axis, start, stop, total=None):
         unroll = 28
@@ -311,12 +317,6 @@
     tables.wait()
     loaded(2)
     begin(3)
-    loaded(0)
-    pl.semaphore_wait(barrier, len(peers))
-    for slots in ((0, 3), (1, 5), (2, 4)):
-        for kind in token_kinds:
-            for slot in slots:
-                token_send(kind, slot)
     carried = products(0, lambda f: x_in[f], wu, 0, 0, 3)
     products(0, lambda f: x_in[f], wu, 0, 3, 6, carried)
     exchange(0, pre_to, pre_ref, pre_in)

time: 80.6 us -> 80.3 us (level)
  no operation moved by 1% of the time
where the time goes in v11:
time: 80.3 us; the launch traced here: 79.7 us
  Pallas kernels  79.1 us (99%)
    pallas_call x1, Pallas kernels, main(): pl.pallas_call(main_kernel, out_shape=[jax.ShapeDtypeStruct((32, ROWS * B...  76.8 us
    pallas_call x1, Pallas kernels, results(): pl.pallas_call(results_kernel, out_shape=[jax.ShapeDtypeStruct(value.shap...  2.23 us

profile of v11, /device:TPU:1, one launch (start us, length us, event | category | flops | bytes accessed | tf_op | source)
XLA Modules:
  0.0 79.7 jit_solution(11998170162026421889)
XLA Ops:
  0.6 76.8 %backward.1 = (bf16[32,3072]{1,0:T(8,128)(2,1)}, bf16[18,128,128]{2,1,0:T(8,128)(2,1)}, bf16[18,128,128]{2,1,0:T(8,128)(2,1)}) custom-call(s32[1,288]{1,0:T(1,128)} %bitcast.9, s32[1,288]{1,0:T(1,128)} %bitcast.10, s32[1,288]{1,0:T(1,128)} %bitcast.11, bf16[128,3072]{1,0:T(8,128)(2,1)} %refs_3_.1, bf16[128,3072]{1,0:T(8,128)(2,1)} %refs_4_.1, ...), custom_call_target="tpu_custom_call" | custom-call | tf_op jit(solution)/shard_map/backward/pallas_call | solution.py:565
  77.5 2.2 %results.1 = (bf16[32,3072]{1,0:T(8,128)(2,1)}, bf16[18,128,128]{2,1,0:T(8,128)(2,1)}, bf16[18,128,128]{2,1,0:T(8,128)(2,1)}) custom-call(bf16[32,3072]{1,0:T(8,128)(2,1)} %get-tuple-element.9.refs_0_, bf16[18,128,128]{2,1,0:T(8,128)(2,1)} %get-tuple-element.10.refs_1_, bf16[18,128,128]{2,1,0:T(8,128)(2,1)} %get-tuple-element.11.refs_2_), custom_call_target="tpu_custom_call" | custom-call | tf_op jit(solution)/shard_map/results/pallas_call | solution.py:598
